TPU v7x, 512 devices: a whole 4x4x16 slice. The times are simulated.
512 devices in a mesh: notes: 64 (over z, y), tensor: 8 (over x, core).
Axes of the slice: x: 4, y: 4, z: 16, core: 2. Of those that a mesh axis runs over, the one named last changes fastest.
Arguments:
- states: bfloat16 [768, 128, 1024], P('notes', None, 'tensor'), may hold values from -128 to 128
- value_weight: bfloat16 [1024, 1024], P(None, 'tensor'), may hold values from -0.1875 to 0.1875
- latent_query: bfloat16 [16, 1024], P(None, 'tensor'), may hold values from -4 to 4
- patient_ids: int32 [768], P('notes'), may hold values from 0 to 63, as said below
- note_order: int32 [768], P('notes'), may hold values from 0 to 17, as said below
- history_length: int32 [64], P('notes'), may hold values from 1 to 18, as said below
- position_table: bfloat16 [18, 1024], P(None, 'tensor'), may hold values from -3 to 3
- attention_gain: float32 [1024], replicated, may hold values from 0.5 to 1.5
- feedforward_gain: float32 [1024], replicated, may hold values from 0.5 to 1.5
- qkv_weight: bfloat16 [1024, 3, 1024], P(None, None, 'tensor'), may hold values from -2 to 2
- out_weight: bfloat16 [1024, 1024], P('tensor'), may hold values from -0.1875 to 0.1875
- up_weight: bfloat16 [1024, 4096], P(None, 'tensor'), may hold values from -0.1875 to 0.1875
- down_weight: bfloat16 [4096, 1024], P('tensor'), may hold values from -0.09375 to 0.09375
- cotangent: bfloat16 [64, 288, 1024], P('notes', None, 'tensor'), may hold values from -6 to 6
Outputs:
- visit_out: bfloat16 [64, 288, 1024], P('notes', None, 'tensor')
- latent_grads: bfloat16 [768, 16, 1024], P('notes', None, 'tensor')
- value_grad: float32 [1024, 1024], P('notes', 'tensor')
- query_grad: float32 [16, 1024], P(None, 'tensor')
Inputs may be any that keep to these rules, and one draw needn't show every extreme that they name: `patient_ids`: patient p's timeline is owned by index p of notes. At most 1 notes held by one index of notes belong to one patient, and some index holds that many for some patient. `note_order`: the notes of patient p carry the numbers 0 to history_length[p] - 1, each once. `history_length`: the lengths sum to 768; the largest is exactly 18.
All inputs are finite; a program needn't handle non-finite values.
Results may differ from a plain program's by a relative error of at most 0.025.
Values may be sent and summed in bfloat16 or wider, within the bound.
A program may use at most 64 MiB of HBM per device.

v0:
```python
import jax
import jax.numpy as jnp
from jax import lax
from jax.sharding import PartitionSpec as P

HEAD = 64


EPSILON = 1e-05
MASKED = -1e30


def norm_rows(values, gain_vector):
    centre = values - jnp.mean(values, axis=-1, keepdims=True)
    inverse = lax.rsqrt(jnp.mean(centre * centre, axis=-1, keepdims=True) + EPSILON)
    scaled = centre * inverse
    return (scaled, inverse, (scaled * gain_vector).astype(jnp.bfloat16))


def norm_back(gradient, scaled, inverse, gain_vector):
    weighted = gradient * gain_vector
    centred = weighted - jnp.mean(weighted, axis=-1, keepdims=True)
    return inverse * (centred - scaled * jnp.mean(weighted * scaled, axis=-1, keepdims=True))


def own_columns(values, local_width):
    return lax.dynamic_slice_in_dim(values, lax.axis_index("tensor") * local_width, local_width, 1)


def project_front(visit_rows, attention_gain, qkv_weight):
    scaled, inverse, normed = norm_rows(visit_rows.astype(jnp.float32), attention_gain)
    flat_weight = qkv_weight.reshape(qkv_weight.shape[0], -1)
    packed = jnp.dot(normed, flat_weight, preferred_element_type=jnp.float32).astype(jnp.bfloat16)
    return (scaled, inverse, packed)


def split_heads(packed, member):
    local_width = packed.shape[1] // 3
    section = packed[:, member * local_width : (member + 1) * local_width]
    return section.reshape(packed.shape[0], local_width // HEAD, HEAD)


def attend(packed, key_valid):
    queries = split_heads(packed, 0)
    keys_all = split_heads(packed, 1)
    values_all = split_heads(packed, 2)
    scores = 0.125 * jnp.einsum(
        "qhe,khe->hqk", queries, keys_all, preferred_element_type=jnp.float32
    )
    scores = jnp.where(key_valid[None, None, :], scores, MASKED)
    probs_full = jax.nn.softmax(scores, axis=-1)
    weights_rounded = probs_full.astype(jnp.bfloat16)
    context = jnp.einsum(
        "hqk,khe->qhe", weights_rounded, values_all, preferred_element_type=jnp.float32
    )
    return (probs_full, weights_rounded, context.astype(jnp.bfloat16).reshape(packed.shape[0], -1))


def attend_back(packed, probs_full, weights_rounded, context_grad):
    queries = split_heads(packed, 0)
    keys_all = split_heads(packed, 1)
    values_all = split_heads(packed, 2)
    grad_heads = context_grad.reshape(queries.shape)
    weight_grad = jnp.einsum(
        "qhe,khe->hqk", grad_heads, values_all, preferred_element_type=jnp.float32
    )
    values_grad = jnp.einsum(
        "hqk,qhe->khe", weights_rounded, grad_heads, preferred_element_type=jnp.float32
    ).astype(jnp.bfloat16)
    score_grad = (
        0.125
        * probs_full
        * (weight_grad - jnp.sum(weight_grad * probs_full, axis=-1, keepdims=True))
    ).astype(jnp.bfloat16)
    queries_grad = jnp.einsum(
        "hqk,khe->qhe", score_grad, keys_all, preferred_element_type=jnp.float32
    ).astype(jnp.bfloat16)
    keys_grad = jnp.einsum(
        "hqk,qhe->khe", score_grad, queries, preferred_element_type=jnp.float32
    ).astype(jnp.bfloat16)
    row_total = packed.shape[0]
    return jnp.concatenate(
        [
            queries_grad.reshape(row_total, -1),
            keys_grad.reshape(row_total, -1),
            values_grad.reshape(row_total, -1),
        ],
        axis=1,
    )


def block_tail(visit_rows, context, feedforward_gain, out_weight, up_weight, down_weight):
    attention = lax.psum(
        jnp.dot(context, out_weight, preferred_element_type=jnp.float32).astype(jnp.bfloat16),
        "tensor",
    ).astype(jnp.float32)
    residual = visit_rows.astype(jnp.float32) + attention
    scaled, inverse, normed = norm_rows(residual, feedforward_gain)
    upper_proj = jnp.dot(normed, up_weight, preferred_element_type=jnp.float32)
    hidden = jax.nn.gelu(upper_proj).astype(jnp.bfloat16)
    feedforward = lax.psum(
        jnp.dot(hidden, down_weight, preferred_element_type=jnp.float32).astype(jnp.bfloat16),
        "tensor",
    ).astype(jnp.float32)
    return (residual + feedforward, (scaled, inverse, upper_proj))


def block_tail_back(output_grad, stored, feedforward_gain, out_weight, up_weight, down_weight):
    scaled, inverse, upper_proj = stored
    hidden_grad = jnp.einsum(
        "rd,fd->rf",
        output_grad.astype(jnp.bfloat16),
        down_weight,
        preferred_element_type=jnp.float32,
    )
    unused, gelu_back = jax.vjp(jax.nn.gelu, upper_proj)
    upper_grad = gelu_back(hidden_grad)[0].astype(jnp.bfloat16)
    normed_grad = lax.psum(
        jnp.einsum("rf,df->rd", upper_grad, up_weight, preferred_element_type=jnp.float32).astype(
            jnp.bfloat16
        ),
        "tensor",
    ).astype(jnp.float32)
    residual_grad = output_grad + norm_back(normed_grad, scaled, inverse, feedforward_gain)
    context_grad = jnp.einsum(
        "rd,fd->rf",
        residual_grad.astype(jnp.bfloat16),
        out_weight,
        preferred_element_type=jnp.float32,
    ).astype(jnp.bfloat16)
    return (residual_grad, context_grad)


def input_back(residual_grad, packed_grad, scaled, inverse, attention_gain, qkv_weight):
    flat_weight = qkv_weight.reshape(qkv_weight.shape[0], -1)
    normed_grad = lax.psum(
        jnp.einsum(
            "rc,dc->rd", packed_grad, flat_weight, preferred_element_type=jnp.float32
        ).astype(jnp.bfloat16),
        "tensor",
    ).astype(jnp.float32)
    return residual_grad + norm_back(normed_grad, scaled, inverse, attention_gain)


def note_routes(patient_ids, note_order, owners, capacity):
    local_total = patient_ids.shape[0]
    positions = jnp.arange(local_total)
    same_patient = patient_ids[:, None] == patient_ids[None, :]
    earlier = positions[:, None] > positions[None, :]
    rank_local = jnp.sum(jnp.where(same_patient & earlier, 1, 0), axis=1)
    owner_match = patient_ids[None, :] == jnp.arange(owners)[:, None]
    slot_match = rank_local[None, :] == jnp.arange(capacity)[:, None]
    selector = (owner_match[:, None, :] & slot_match[None, :, :]).astype(jnp.bfloat16)
    order_codes = jnp.einsum(
        "pcj,j->pc",
        selector,
        (note_order + 1).astype(jnp.bfloat16),
        preferred_element_type=jnp.float32,
    )
    return (selector, order_codes.astype(jnp.bfloat16))


def pack_rows(selector, flat_rows):
    return jnp.einsum(
        "pcj,jf->pcf", selector, flat_rows, preferred_element_type=jnp.float32
    ).astype(jnp.bfloat16)


def unpack_rows(selector, arrived):
    return jnp.einsum("pcj,pcf->jf", selector, arrived, preferred_element_type=jnp.float32).astype(
        jnp.bfloat16
    )


def owner_slots(order_codes, most_notes):
    flat_codes = order_codes.reshape(-1)
    targets = jnp.arange(1, most_notes + 1).astype(jnp.bfloat16)
    return (flat_codes[None, :] == targets[:, None]).astype(jnp.bfloat16)


def owner_gather(placement, arrived):
    flat_arrived = arrived.reshape(placement.shape[1], -1)
    return jnp.dot(placement, flat_arrived, preferred_element_type=jnp.float32).astype(jnp.bfloat16)


def owner_send(placement, slot_rows, owners):
    outgoing = jnp.einsum(
        "ms,mf->sf", placement, slot_rows, preferred_element_type=jnp.float32
    ).astype(jnp.bfloat16)
    return outgoing.reshape(owners, -1, slot_rows.shape[1])


def shards(
    states,
    value_weight,
    latent_query,
    patient_ids,
    note_order,
    history_length,
    position_table,
    attention_gain,
    feedforward_gain,
    qkv_weight,
    out_weight,
    up_weight,
    down_weight,
    cotangent,
):
    note_count, token_count, local_width = states.shape
    latent_count = latent_query.shape[0]
    most_notes = position_table.shape[0]
    history = most_notes * latent_count
    owners = lax.axis_size("notes")
    capacity = (most_notes + owners - 1) // owners
    local_heads = local_width // HEAD
    note_width = latent_count * local_width
    full_states = lax.all_gather(states, "tensor", axis=2, tiled=True)
    pool_values = jnp.einsum(
        "ntd,dk->ntk", full_states, value_weight, preferred_element_type=jnp.float32
    )
    pool_values = pool_values.astype(jnp.bfloat16)
    state_heads = states.reshape(note_count, token_count, local_heads, HEAD)
    value_heads = pool_values.reshape(note_count, token_count, local_heads, HEAD)
    query_heads = latent_query.reshape(latent_count, local_heads, HEAD)
    pool_scores = 0.125 * jnp.einsum(
        "lhe,nthe->nhlt", query_heads, state_heads, preferred_element_type=jnp.float32
    )
    pool_probs = jax.nn.softmax(pool_scores, axis=-1)
    pool_weights = pool_probs.astype(jnp.bfloat16)
    pooled = jnp.einsum(
        "nhlt,nthe->nlhe", pool_weights, value_heads, preferred_element_type=jnp.float32
    )
    pooled = pooled.astype(jnp.bfloat16).reshape(note_count, note_width)
    selector, order_codes = note_routes(patient_ids, note_order, owners, capacity)
    key_valid = jnp.arange(history) < history_length[0] * latent_count
    row_valid = key_valid[:, None]
    arrived, arrived_codes = (
        lax.all_to_all(
            pack_rows(selector, pooled), "notes", split_axis=0, concat_axis=0, tiled=True
        ),
        lax.all_to_all(order_codes, "notes", split_axis=0, concat_axis=0, tiled=True),
    )
    placement = owner_slots(arrived_codes, most_notes)
    placed = owner_gather(placement, arrived).reshape(history, local_width)
    position_rows = jnp.repeat(position_table, latent_count, axis=0)
    visit_local = jnp.where(
        row_valid, placed.astype(jnp.float32) + position_rows.astype(jnp.float32), 0.0
    ).astype(jnp.bfloat16)
    visit_rows, cotangent_rows = (
        lax.all_gather(visit_local, "tensor", axis=1, tiled=True),
        lax.all_gather(cotangent[0], "tensor", axis=1, tiled=True),
    )
    scaled, inverse, packed = project_front(visit_rows, attention_gain, qkv_weight)
    probs_full, weights_rounded, context = attend(packed, key_valid)
    output_full, stored = block_tail(
        visit_rows, context, feedforward_gain, out_weight, up_weight, down_weight
    )
    visit_out = jnp.where(row_valid, own_columns(output_full, local_width), 0.0).astype(
        jnp.bfloat16
    )
    output_grad = jnp.where(row_valid, cotangent_rows.astype(jnp.float32), 0.0)
    residual_grad, context_grad = block_tail_back(
        output_grad, stored, feedforward_gain, out_weight, up_weight, down_weight
    )
    packed_grad = attend_back(packed, probs_full, weights_rounded, context_grad)
    visit_grad = input_back(residual_grad, packed_grad, scaled, inverse, attention_gain, qkv_weight)
    slot_grads = (
        own_columns(visit_grad, local_width).astype(jnp.bfloat16).reshape(most_notes, note_width)
    )
    returned = lax.all_to_all(
        owner_send(placement, slot_grads, owners), "notes", split_axis=0, concat_axis=0, tiled=True
    )
    latent_grads = unpack_rows(selector, returned)
    grad_heads = latent_grads.reshape(note_count, latent_count, local_heads, HEAD)
    values_grad = jnp.einsum(
        "nhlt,nlhe->nthe", pool_weights, grad_heads, preferred_element_type=jnp.float32
    )
    values_grad = values_grad.astype(jnp.bfloat16).reshape(note_count, token_count, local_width)
    value_grad = lax.psum_scatter(
        jnp.einsum("ntd,ntk->dk", full_states, values_grad, preferred_element_type=jnp.float32),
        "notes",
        scatter_dimension=0,
        tiled=True,
    )
    prob_grad = jnp.einsum(
        "nlhe,nthe->nhlt", grad_heads, value_heads, preferred_element_type=jnp.float32
    )
    score_grad = (
        pool_probs * (prob_grad - jnp.sum(prob_grad * pool_probs, axis=-1, keepdims=True))
    ).astype(jnp.bfloat16)
    query_partial = 0.125 * jnp.einsum(
        "nhlt,nthe->lhe", score_grad, state_heads, preferred_element_type=jnp.float32
    )
    query_grad = lax.psum(query_partial.reshape(latent_count, local_width), "notes")
    return (
        visit_out[None],
        latent_grads.reshape(note_count, latent_count, local_width),
        value_grad,
        query_grad,
    )


def solution(mesh):
    return jax.shard_map(
        shards,
        mesh=mesh,
        in_specs=(
            P("notes", None, "tensor"),
            P(None, "tensor"),
            P(None, "tensor"),
            P("notes"),
            P("notes"),
            P("notes"),
            P(None, "tensor"),
            P(),
            P(),
            P(None, None, "tensor"),
            P("tensor", None),
            P(None, "tensor"),
            P("tensor", None),
            P("notes", None, "tensor"),
        ),
        out_specs=(
            P("notes", None, "tensor"),
            P("notes", None, "tensor"),
            P("notes", "tensor"),
            P(None, "tensor"),
        ),
        check_vma=False,
    )
```

profile of v0, /device:TPU:1, one launch (start us, length us, event | category | flops | bytes accessed | tf_op | source)
XLA Modules:
  0.0 1076.6 jit_solution(13888831742560875637)
XLA Ops:
  7.9 0.9 select_reduce_fusion
  8.9 0.8 fusion.21
  10.4 19.3 %all-to-all-start = ((bf16[64,1,1]{2,1,0:T(2,128)(2,1)}), bf16[64,1,1]{2,1,0:T(2,128)(2,1)S(1)}, u32[]{:S(2)}, u32[]{:S(2)}) async-start(bf16[64,1,1]{2,1,0:T(2,128)(2,1)} %copy.116), calls=%async_computation | async-start | bytes 65536 | tf_op jit(solution)/shard_map/all_to_all | solution.py:241
  29.7 1.2 copy.118
  31.9 3.9 fusion.132
  35.8 19.5 %all-gather.3.cloned.1.call-done = bf16[12,128,1024]{2,1,0:T(8,128)(2,1)} async-done(((bf16[12,128,128]{2,1,0:T(8,128)(2,1)}), bf16[12,128,1024]{2,1,0:T(8,128)(2,1)}) %all-gather.3.cloned.1.call-update) | async-done | bytes 3145744 | tf_op jit(solution)/shard_map/all_gather | solution.py:217
  55.2 3.1 convolution_convert_fusion.9
  61.3 0.9 reshape.277
  62.2 15.3 %all-to-all-start.1 = ((bf16[64,2,1024]{2,1,0:T(2,128)(2,1)}), bf16[64,2,1024]{2,1,0:T(2,128)(2,1)S(1)}, u32[]{:S(2)}, u32[]{:S(2)}) async-start(bf16[64,2,1024]{2,1,0:T(2,128)(2,1)} %reshape.277), calls=%async_computation.1 | async-start | bytes 524288 | tf_op jit(solution)/shard_map/all_to_all | solution.py:238
  79.1 18.7 %all-to-all-done.1 = bf16[64,2,1024]{2,1,0:T(2,128)(2,1)S(1)} async-done(((bf16[64,2,1024]{2,1,0:T(2,128)(2,1)}), bf16[64,2,1024]{2,1,0:T(2,128)(2,1)S(1)}, u32[]{:S(2)}, u32[]{:S(2)}) %all-to-all-start.1) | async-done | bytes 262176 | tf_op jit(solution)/shard_map/all_to_all | solution.py:238
  98.5 16.1 %all_gather.10 = bf16[288,1024]{1,0:T(8,128)(2,1)S(1)} all-gather(bf16[288,128]{1,0:T(8,128)(2,1)S(1)} %fusion.82), channel_id=1, replica_groups=mesh['notes'=64,'tensor'=8] {'tensor'}, dimensions={1}, use_global_device_ids=true | all-gather | bytes 663552 | tf_op jit(solution)/shard_map/all_gather | solution.py:250
  116.1 1.4 fusion.133
  118.5 1.2 convolution_convert_fusion.4
  119.7 12.8 %all-gather = bf16[1,288,1024]{2,1,0:T(8,128)(2,1)S(1)} all-gather(bf16[1,288,128]{2,1,0:T(8,128)(2,1)S(1)} %copy-done.23), channel_id=2, replica_groups=mesh['notes'=64,'tensor'=8] {'tensor'}, dimensions={2}, use_global_device_ids=true | all-gather | bytes 663552 | tf_op jit(solution)/shard_map/all_gather | solution.py:251
  132.5 51.3 %all-reduce.5.cloned.1.call-done = bf16[288,1024]{1,0:T(8,128)(2,1)} async-done(((bf16[288,1024]{1,0:T(8,128)(2,1)}), bf16[288,1024]{1,0:T(8,128)(2,1)}) %all-reduce.5.cloned.1.call-update) | async-done | bytes 589840 | tf_op jit(solution)/shard_map/psum | solution.py:93
  183.8 1.4 fusion.129
  186.2 3.2 convolution_convert_fusion.6
  189.6 1.4 convolution_convert_fusion.7
  191.0 74.4 %all-reduce.7.cloned.1.call-done = bf16[288,1024]{1,0:T(8,128)(2,1)} async-done(((bf16[288,1024]{1,0:T(8,128)(2,1)}), bf16[288,1024]{1,0:T(8,128)(2,1)}) %all-reduce.7.cloned.1.call-update) | async-done | bytes 589840 | tf_op jit(solution)/shard_map/psum | solution.py:118
  265.4 1.6 fusion.13
  267.1 1.5 fusion.11
  269.5 1.6 multiply_reduce_fusion.3
  273.2 2.4 convolution_convert_fusion.5
  275.7 77.7 %all-reduce.9.cloned.1.call-done = (bf16[288,1024]{1,0:T(8,128)(2,1)}, bf16[288,1024]{1,0:T(8,128)(2,1)}) async-done(((bf16[288,1024]{1,0:T(8,128)(2,1)}, bf16[288,1024]{1,0:T(8,128)(2,1)}), (bf16[288,1024]{1,0:T(8,128)(2,1)}, bf16[288,1024]{1,0:T(8,128)(2,1)})) %all-reduce.9.cloned.1.call-update) | async-done | bytes 1179664 | tf_op jit(solution)/shard_map/psum | solution.py:101
  353.4 1.5 fusion.48
  356.5 32.4 %all_to_all.19 = bf16[64,2,1024]{2,1,0:T(2,128)(2,1)S(1)} all-to-all(bf16[64,2,1024]{2,1,0:T(2,128)(2,1)S(1)} %reshape.279), channel_id=1, replica_groups=mesh['notes'=64,'tensor'=8] {'notes'}, dimensions={0} | all-to-all | bytes 524288 | tf_op jit(solution)/shard_map/all_to_all | solution.py:270
  390.0 2.5 convolution_bitcast_fusion
  392.5 1.0 copy.156
  393.5 1.8 fusion.88
  395.6 0.8 fusion.19
  397.2 114.8 %psum.39 = f32[16,128]{1,0:T(8,128)} all-reduce(f32[16,128]{1,0:T(8,128)S(1)} %reshape.264), channel_id=1, replica_groups=mesh['notes'=64,'tensor'=8] {'notes'}, use_global_device_ids=true, to_apply=%region_20.21 | all-reduce | flops 2048 | bytes 16384 | tf_op jit(solution)/shard_map/psum | solution.py:294
  512.0 558.0 %reduce-scatter.4.cloned.1.call-done = f32[16,128]{1,0:T(8,128)} async-done(((f32[1024,128]{1,0:T(8,128)}), f32[16,128]{1,0:T(8,128)}) %reduce-scatter.4.cloned.1.call-update) | async-done | bytes 8208
  (141 shorter events, 17.1 us)
Async XLA Ops:
  7.2 179.0 %copy-start = (bf16[512,1024]{1,0:T(8,128)(2,1)S(1)}, bf16[512,1024]{1,0:T(8,128)(2,1)}, u32[]{:S(2)}) copy-start(bf16[512,1024]{1,0:T(8,128)(2,1)} %param.26) | copy-start | bytes 3145732
  7.2 23.7 %copy-start.26 = (bf16[16,128]{1,0:T(8,128)(2,1)S(1)}, bf16[16,128]{1,0:T(8,128)(2,1)}, u32[]{:S(2)}) copy-start(bf16[16,128]{1,0:T(8,128)(2,1)} %param.16) | copy-start | bytes 12292
  7.2 48.1 %copy-start.18 = (bf16[1024,128]{1,0:T(8,128)(2,1)S(1)}, bf16[1024,128]{1,0:T(8,128)(2,1)}, u32[]{:S(2)}) copy-start(bf16[1024,128]{1,0:T(8,128)(2,1)} %param.15) | copy-start | bytes 786436
  7.2 48.0 %all-gather.3.cloned.1.call-start = ((), (), s32[]{:S(2)}) async-start(), calls=%async_computation.4 | async-start | bytes 3538944 | tf_op jit(solution)/shard_map/all_gather | solution.py:217
  8.9 50.8 %copy-start.32 = (pred[12]{0:T(512)(128)(4,1)}, pred[12]{0:T(512)(128)(4,1)S(1)}, u32[]{:S(2)}) copy-start(pred[12]{0:T(512)(128)(4,1)S(1)} %broadcast_compare_fusion) | copy-start | bytes 40
  10.4 51.8 %all-to-all-start = ((bf16[64,1,1]{2,1,0:T(2,128)(2,1)}), bf16[64,1,1]{2,1,0:T(2,128)(2,1)S(1)}, u32[]{:S(2)}, u32[]{:S(2)}) async-start(bf16[64,1,1]{2,1,0:T(2,128)(2,1)} %copy.116), calls=%async_computation | async-start | bytes 65536 | tf_op jit(solution)/shard_map/all_to_all | solution.py:241
  30.9 27.4 %copy-start.5 = (bf16[12,128,128]{1,2,0:T(8,128)(2,1)}, bf16[12,128,128]{1,2,0:T(8,128)(2,1)S(1)}, u32[]{:S(2)}) copy-start(bf16[12,128,128]{1,2,0:T(8,128)(2,1)S(1)} %copy.118) | copy-start | bytes 1179652
  35.8 22.6 %copy-start.19 = (f32[12,2,16,128]{3,2,0,1:T(8,128)}, f32[12,2,16,128]{3,2,0,1:T(8,128)S(1)}, u32[]{:S(2)}) copy-start(f32[12,2,16,128]{3,2,0,1:T(8,128)S(1)} %get-tuple-element.38) | copy-start | bytes 589828
  59.4 18.8 %copy-start.25 = (bf16[18,128]{1,0:T(8,128)(2,1)S(1)}, bf16[18,128]{1,0:T(8,128)(2,1)}, u32[]{:S(2)}) copy-start(bf16[18,128]{1,0:T(8,128)(2,1)} %param.20) | copy-start | bytes 13828
  59.4 18.8 %copy-start.10 = (bf16[1024,3,128]{2,0,1:T(8,128)(2,1)S(1)}, bf16[1024,3,128]{2,0,1:T(8,128)(2,1)}, u32[]{:S(2)}) copy-start(bf16[1024,3,128]{2,0,1:T(8,128)(2,1)} %param.23) | copy-start | bytes 2359300
  62.2 35.6 %all-to-all-start.1 = ((bf16[64,2,1024]{2,1,0:T(2,128)(2,1)}), bf16[64,2,1024]{2,1,0:T(2,128)(2,1)S(1)}, u32[]{:S(2)}, u32[]{:S(2)}) async-start(bf16[64,2,1024]{2,1,0:T(2,128)(2,1)} %reshape.277), calls=%async_computation.1 | async-start | bytes 524288 | tf_op jit(solution)/shard_map/all_to_all | solution.py:238
  77.5 106.3 %all-reduce.5.cloned.1.call-start = ((), (), s32[]{:S(2)}) async-start(), calls=%async_computation.5 | async-start | bytes 1179648 | tf_op jit(solution)/shard_map/psum | solution.py:93
  78.5 36.6 %copy-start.11 = (bf16[1024,3,128]{0,2,1:T(8,128)(2,1)}, bf16[1024,3,128]{0,2,1:T(8,128)(2,1)S(1)}, u32[]{:S(2)}) copy-start(bf16[1024,3,128]{0,2,1:T(8,128)(2,1)S(1)} %copy.124) | copy-start | bytes 2359300
  78.6 36.1 %copy-start.34 = (bf16[18]{0:T(256)(128)(2,1)}, bf16[18]{0:T(256)(128)(2,1)S(1)}, u32[]{:S(2)}) copy-start(bf16[18]{0:T(256)(128)(2,1)S(1)} %add_convert_fusion) | copy-start | bytes 112
  98.4 16.8 %copy-start.27 = (f32[1024]{0:T(1024)S(1)}, f32[1024]{0:T(1024)}, u32[]{:S(2)}) copy-start(f32[1024]{0:T(1024)} %param.21) | copy-start | bytes 12292
  116.0 2.1 copy-start.16
  116.1 2.0 copy-start.21
  119.7 145.7 %all-reduce.7.cloned.1.call-start = ((), (), s32[]{:S(2)}) async-start(), calls=%async_computation.6 | async-start | bytes 1179648 | tf_op jit(solution)/shard_map/psum | solution.py:118
  132.5 53.7 %copy-start.3 = (bf16[1,288,1024]{2,1,0:T(8,128)(2,1)}, bf16[1,288,1024]{2,1,0:T(8,128)(2,1)S(1)}, u32[]{:S(2)}) copy-start(bf16[1,288,1024]{2,1,0:T(8,128)(2,1)S(1)} %all-gather) | copy-start | bytes 1769476
  132.5 53.1 %copy-start.24 = (f32[1024]{0:T(1024)S(1)}, f32[1024]{0:T(1024)}, u32[]{:S(2)}) copy-start(f32[1024]{0:T(1024)} %param.22) | copy-start | bytes 12292
  183.8 1.8 copy-start.36
  189.4 163.9 %all-reduce.9.cloned.1.call-start = ((), (), s32[]{:S(2)}) async-start(), calls=%async_computation.8 | async-start | bytes 2359296 | tf_op jit(solution)/shard_map/psum | solution.py:101
  265.4 1.7 copy-start.2
  265.4 1.7 copy-start.4
  275.6 794.4 %reduce-scatter.4.cloned.1.call-start = ((), (), s32[]{:S(2)}) async-start(), calls=%async_computation.7 | async-start | bytes 532480
  353.4 1.8 copy-start.35
  355.5 33.7 %copy-start.31 = (s32[12]{0:T(128)S(1)}, s32[12]{0:T(128)}, u32[]{:S(2)}) copy-start(s32[12]{0:T(128)} %param.17) | copy-start | bytes 148
  355.5 33.7 %copy-start.33 = (pred[12]{0:T(512)(128)(4,1)S(1)}, pred[12]{0:T(512)(128)(4,1)}, u32[]{:S(2)}) copy-start(pred[12]{0:T(512)(128)(4,1)} %copy-done.32) | copy-start | bytes 40
  356.3 33.3 %copy-start.20 = (f32[12,2,16,128]{3,2,0,1:T(8,128)S(1)}, f32[12,2,16,128]{3,2,0,1:T(8,128)}, u32[]{:S(2)}) copy-start(f32[12,2,16,128]{3,2,0,1:T(8,128)} %copy-done.19) | copy-start | bytes 589828
  392.5 2.8 copy-start.15
  393.5 2.1 copy-start.6
  393.5 2.1 copy-start.13
  (12 other events, 13.2 us)
Sparse Core Ops, SparseCore 0:
  10.2 45.0 all-gather.2
  119.8 64.0 all-reduce.4
  189.5 75.7 all-reduce.6
  275.7 77.5 all-reduce.8
  393.7 676.3 reduce-scatter.3
where the time goes:
time: 1090 us; the launch traced here: 1080 us
  waiting for transfers between devices  800 us (73%)
  blocking collectives  176 us (16%)
  starting transfers between devices  34.9 us (3%)
  matrix products  23.9 us (2%)
  other arithmetic  16.1 us (1%)
  between operations  15.1 us (1%)
    unnamed x6, waiting for transfers between devices  559 us
    psum x1, blocking collectives, shards(): lax.psum(query_partial.reshape(latent_count, local_width), 'notes')  115 us
    psum x1, waiting for transfers between devices, block_tail(): lax.psum(jnp.dot(hidden, down_weight, preferred_element_type=jnp.float32)...  77.7 us
    psum x1, waiting for transfers between devices, block_tail_back(): lax.psum(jnp.einsum('rf,df->rd', upper_grad, up_weight, preferred_element...  74.4 us
    psum x1, waiting for transfers between devices, block_tail(): lax.psum(jnp.dot(context, out_weight, preferred_element_type=jnp.float32)...  51.3 us
    all_to_all x1, blocking collectives, shards(): lax.all_to_all(owner_send(placement, slot_grads, owners), 'notes', split_...  32.4 us
  transfers between devices with their start and end apart: 7, of which 6 were waited for; matrix products, arithmetic and copies ran while one was open for 2% of the time, Pallas kernels for 0%

commit v1 on v0

v1 whole, which is shorter than its diff:
```python
import functools

import jax
import jax.numpy as jnp
from jax import lax
from jax.experimental import pallas as pl
from jax.experimental.pallas import tpu as pltpu
from jax.sharding import PartitionSpec as P

HEAD = 64
EPSILON = 1e-05
MASKED = -1e30
MESH = pl.DeviceIdType.MESH
F32 = jnp.float32
BF16 = jnp.bfloat16
I32 = jnp.int32


def remote(src, dst, send, recv, device):
    return pltpu.make_async_remote_copy(
        src_ref=src,
        dst_ref=dst,
        send_sem=send,
        recv_sem=recv,
        device_id=device,
        device_id_type=MESH,
    )


def dot_nn(a, b):
    return lax.dot_general(a, b, (((1,), (0,)), ((), ())), preferred_element_type=F32)


def dot_nt(a, b):
    return lax.dot_general(a, b, (((1,), (1,)), ((), ())), preferred_element_type=F32)


def dot_tn(a, b):
    return lax.dot_general(a, b, (((0,), (0,)), ((), ())), preferred_element_type=F32)


def iota(shape, dim):
    return lax.broadcasted_iota(I32, shape, dim)


class Place:
    def __init__(self, nt):
        self.nt = nt
        self.nx = nt // 2
        self.me = lax.axis_index("tensor")
        self.x = self.me // 2
        self.c = lax.rem(self.me, 2)
        self.sibling = self.at(0, 1)

    def at(self, step, flip):
        core = 1 - self.c if flip else self.c
        return lax.rem(self.x + step, self.nx) * 2 + core


class RingGather:
    def __init__(self, place, src, full, send, recv):
        self.place, self.src, self.full, self.send, self.recv = place, src, full, send, recv
        self.half = src.shape[0] // 2
        self.copies = []

    def part(self, ref, j):
        return ref.at[pl.ds(j * self.half, self.half)]

    def copy(self, src, owner, j, to):
        one = remote(
            src,
            self.part(self.full.at[owner], j),
            self.send.at[len(self.copies)],
            self.recv.at[owner, j],
            {"tensor": to},
        )
        one.start()
        self.copies.append(one)

    def arrive(self, owner, j):
        remote(
            self.part(self.src, j),
            self.part(self.full.at[owner], j),
            self.send.at[0],
            self.recv.at[owner, j],
            {"tensor": owner},
        ).wait_recv()

    def start(self):
        p = self.place
        right, left = p.at(1, 0), p.at(3, 0)
        for j, to in ((0, right), (1, left), (1, right), (0, left), (0, p.sibling), (1, p.sibling)):
            self.copy(self.part(self.src, j), p.me, j, to)
        self.full[p.me] = self.src[...]

    def pass_on(self):
        p = self.place
        right, left = p.at(1, 0), p.at(3, 0)
        for owner, j, to in ((left, 0, right), (right, 1, left)):
            self.arrive(owner, j)
            self.copy(self.part(self.full.at[owner], j), owner, j, to)
            self.copy(self.part(self.full.at[owner], j), owner, j, p.sibling)

    def relay_near(self):
        p = self.place
        for owner, j in ((p.at(3, 0), 1), (p.at(1, 0), 0)):
            self.arrive(owner, j)
            self.copy(self.part(self.full.at[owner], j), owner, j, p.sibling)

    def relay_far(self):
        p = self.place
        for j in range(2):
            self.arrive(p.at(2, 0), j)
            self.copy(self.part(self.full.at[p.at(2, 0)], j), p.at(2, 0), j, p.sibling)

    def finish(self):
        for step in (0, 1, 3, 2):
            for j in range(2):
                self.arrive(self.place.at(step, 1), j)
        for one in self.copies:
            one.wait_send()


class RelayGather:
    def __init__(self, place, src, full, send, recv):
        self.place, self.src, self.full, self.send, self.recv = place, src, full, send, recv
        self.copies = []

    def copy(self, src, owner, to):
        one = remote(
            src,
            self.full.at[owner],
            self.send.at[len(self.copies)],
            self.recv.at[owner],
            {"tensor": to},
        )
        one.start()
        self.copies.append(one)

    def arrive(self, owner):
        remote(
            self.src, self.full.at[owner], self.send.at[0], self.recv.at[owner], {"tensor": owner}
        ).wait_recv()

    def start(self):
        p = self.place
        for to in (p.at(2, 0), p.at(1, 0), p.at(3, 0), p.sibling):
            self.copy(self.src, p.me, to)
        self.full[p.me] = self.src[...]

    def finish(self):
        p = self.place
        for step in (1, 3, 2):
            owner = p.at(step, 0)
            self.arrive(owner)
            self.copy(self.full.at[owner], owner, p.sibling)
        for step in (0, 1, 3, 2):
            self.arrive(p.at(step, 1))

    def drain(self):
        for one in self.copies:
            one.wait_send()


class Exchange:
    def __init__(self, place, src, slots, send, recv, same=False):
        self.place, self.src, self.slots, self.send, self.recv = place, src, slots, send, recv
        self.copies = []
        self.same = same

    def block(self, t):
        return self.src if self.same else self.src.at[t]

    def start(self):
        p = self.place
        for k in range(1, p.nt):
            to = lax.rem(p.me + k, p.nt)
            one = remote(
                self.block(to),
                self.slots.at[p.me],
                self.send.at[k - 1],
                self.recv.at[p.me],
                {"tensor": to},
            )
            one.start()
            self.copies.append(one)
        self.slots[p.me] = self.block(p.me)[...]

    def finish(self):
        p = self.place
        for k in range(1, p.nt):
            owner = lax.rem(p.me + k, p.nt)
            remote(
                self.block(owner),
                self.slots.at[owner],
                self.send.at[0],
                self.recv.at[owner],
                {"tensor": owner},
            ).wait_recv()

    def drain(self):
        for one in self.copies:
            one.wait_send()


class AllToAll:
    def __init__(self, count, src, slots, send, recv):
        self.count, self.src, self.slots, self.send, self.recv = count, src, slots, send, recv
        self.me = lax.axis_index("notes")

    def start(self):
        def step(k, carry):
            to = lax.rem(self.me + k, self.count)
            remote(
                self.src.at[to], self.slots.at[self.me], self.send, self.recv, {"notes": to}
            ).start()
            return carry

        lax.fori_loop(1, self.count, step, 0)
        self.slots[self.me] = self.src[self.me]

    def finish(self):
        span = pl.ds(0, self.count - 1)
        remote(
            self.src.at[span], self.slots.at[span], self.send, self.recv, {"notes": self.me}
        ).wait()


def norm_rows(values, gain):
    centre = values - jnp.mean(values, axis=-1, keepdims=True)
    inverse = lax.rsqrt(jnp.mean(centre * centre, axis=-1, keepdims=True) + EPSILON)
    scaled = centre * inverse
    return scaled, inverse, (scaled * gain).astype(BF16)


def side_by_side(blocks):
    return jnp.concatenate([blocks[t] for t in range(blocks.shape[0])], axis=1)


def body(
    dims,
    pid,
    order,
    length,
    states,
    lq,
    pos,
    gain1,
    gain2,
    cot,
    outw,
    wv_hbm,
    qkv_hbm,
    up_hbm,
    down_hbm,
    visit_out,
    latent_out,
    value_out,
    query_out,
    wv,
    qkv,
    up,
    down,
    full,
    cotf,
    outf,
    codes_out,
    codes_in,
    probs,
    weights,
    values,
    mixture,
    slots,
    arrived,
    place_t,
    place,
    vloc,
    visitf,
    scaled1,
    inverse1,
    projected,
    vprobs,
    ctxl,
    ctxf,
    residual_own,
    hidden_grad,
    part2,
    got2,
    sum2,
    sum2f,
    partf,
    gotf,
    rgrad,
    part1,
    got1,
    stat,
    stats,
    slots2,
    arrived2,
    vpart,
    vgot,
    vpart2,
    vgot2,
    qpart,
    qgot,
    qpart2,
    qgot2,
    load_sem,
    ring_send,
    ring_recv,
    relay_send,
    relay_recv,
    ex_send,
    ex_recv,
    a2a_send,
    a2a_recv,
    y_send,
    y_recv,
    z_send,
    z_recv,
):
    nn, ny, nt, notes, tok, lat, most = dims
    nz = nn // ny
    rows = most * lat
    width = 128
    tp = Place(nt)
    who = lax.axis_index("notes")
    wz, wy = who // ny, lax.rem(who, ny)

    barrier = pltpu.get_barrier_semaphore()

    def greet(k, carry):
        pl.semaphore_signal(
            barrier, inc=1, device_id={"notes": lax.rem(who + k, nn)}, device_id_type=MESH
        )
        return carry

    for k in range(1, nt):
        pl.semaphore_signal(
            barrier, inc=1, device_id={"tensor": lax.rem(tp.me + k, nt)}, device_id_type=MESH
        )
    lax.fori_loop(1, nn, greet, 0)
    loads = [
        pltpu.make_async_copy(src, dst, load_sem.at[i])
        for i, (src, dst) in enumerate(((wv_hbm, wv), (qkv_hbm, qkv), (up_hbm, up), (down_hbm, down)))
    ]
    for one in loads:
        one.start()
    pl.semaphore_wait(barrier, nt - 1 + nn - 1)

    ring_states = RingGather(tp, states, full, ring_send.at[0], ring_recv.at[0])
    ring_cot = RingGather(tp, cot, cotf, ring_send.at[1], ring_recv.at[1])
    ring_out = RingGather(tp, outw, outf, ring_send.at[2], ring_recv.at[2])
    ring_states.start()

    patient = iota((nn, 1, width), 0)
    codes = jnp.zeros((nn, 1, width), I32)
    for n in range(notes):
        codes = jnp.where(patient == pid[n], order[n] + 1, codes)
    codes_out[...] = codes
    route = AllToAll(nn, codes_out, codes_in, a2a_send.at[0], a2a_recv.at[0])
    route.start()

    low = (iota((1, width), 1) < HEAD).astype(F32)
    low_b, high_b = low.astype(BF16), (1.0 - low).astype(BF16)
    query = jnp.concatenate([lq[...] * low_b, lq[...] * high_b], axis=0)
    both = 2 * lat
    for n in range(notes):
        score = 0.125 * dot_nt(query, states[n * tok : (n + 1) * tok, :])
        score = jnp.exp(score - jnp.max(score, axis=-1, keepdims=True))
        prob = score / jnp.sum(score, axis=-1, keepdims=True)
        probs[n * both : (n + 1) * both, :] = prob
        weights[n * both : (n + 1) * both, :] = prob.astype(BF16)

    ring_states.pass_on()
    ring_states.relay_near()
    ring_cot.start()
    ring_out.start()
    ring_states.relay_far()
    ring_states.finish()

    loads[0].wait()
    pooled = []
    lane_low = iota((lat, width), 1) < HEAD
    for n in range(notes):
        here = pl.ds(n * tok, tok)
        note = jnp.concatenate([full[t, here, :] for t in range(nt)], axis=1)
        value = dot_nn(note, wv[...]).astype(BF16)
        values[here, :] = value
        mix = dot_nn(weights[n * both : (n + 1) * both, :], value)
        pooled.append(jnp.where(lane_low, mix[:lat], mix[lat:]))
    pooled = jnp.concatenate(pooled, axis=0).astype(BF16)

    line = iota((1, notes * lat), 1)
    target = lax.rem(line, lat)
    for n in range(notes):
        target = jnp.where(line // lat == n, target + pid[n] * lat, target)
    select = (iota((nn * lat, notes * lat), 0) == target).astype(F32).astype(BF16)
    slots[...] = dot_nn(select, pooled).astype(BF16).reshape(nn, lat, width)
    forward = AllToAll(nn, slots, arrived, a2a_send.at[1], a2a_recv.at[1])
    forward.start()

    ring_cot.pass_on()
    ring_out.pass_on()
    ring_cot.relay_near()
    ring_out.relay_near()
    ring_cot.relay_far()
    ring_out.relay_far()

    route.finish()
    code = jnp.broadcast_to(codes_in[...], (nn, lat, width)).reshape(nn * lat, width)
    slot_row = jnp.where(code > 0, (code - 1) * lat + lax.rem(iota((nn * lat, width), 0), lat), -1)
    padded = place_t.shape[1]
    placing = jnp.concatenate(
        [
            (iota((nn * lat, width), 1) + j * width == slot_row).astype(F32)
            for j in range(padded // width)
        ],
        axis=1,
    )
    place_t[...] = placing.astype(BF16)
    place[...] = jnp.transpose(placing).astype(BF16)

    for n in range(notes):
        here = pl.ds(n * tok, tok)
        note = jnp.concatenate([full[t, here, :] for t in range(nt)], axis=1)
        mixed = dot_nn(weights[n * both : (n + 1) * both, :], note)
        mixture[n * both : (n + 1) * both, :] = mixed.astype(BF16)

    limit = length[0] * lat
    row_valid = iota((rows, width), 0) < limit
    positions = pos[...].astype(F32)
    positions = jnp.concatenate(
        [jnp.broadcast_to(positions[m : m + 1, :], (lat, width)) for m in range(most)], axis=0
    )
    ring_cot.finish()
    ring_out.finish()
    loads[1].wait()
    loads[2].wait()
    loads[3].wait()
    out_grad = jnp.where(iota((rows, nt * width), 0) < limit, side_by_side(cotf).astype(F32), 0.0)
    hidden_grad[...] = dot_nt(out_grad.astype(BF16), down[...])

    forward.finish()
    placed = dot_nn(place[...], arrived[...].reshape(nn * lat, width))[:rows]
    vloc[...] = jnp.where(row_valid, placed + positions, 0.0).astype(BF16)

    gather1 = RelayGather(tp, vloc, visitf, relay_send.at[0], relay_recv.at[0])
    gather1.start()
    gather1.finish()
    visit = side_by_side(visitf).astype(F32)
    scaled, inverse, normed = norm_rows(visit, gain1[...])
    scaled1[...] = scaled
    inverse1[...] = jnp.broadcast_to(inverse, (rows, width))
    projected[...] = dot_nn(normed, qkv[...]).astype(BF16)
    q, k, v = (projected[:, j * width : (j + 1) * width] for j in range(3))
    key_valid = iota((1, rows), 1) < limit
    contexts = []
    for h, mask in enumerate((low_b, high_b)):
        score = jnp.where(key_valid, 0.125 * dot_nt(q, k * mask), MASKED)
        score = jnp.exp(score - jnp.max(score, axis=-1, keepdims=True))
        prob = score / jnp.sum(score, axis=-1, keepdims=True)
        vprobs[h] = prob
        contexts.append(dot_nn(prob.astype(BF16), v))
    row_low = iota((rows, width), 1) < HEAD
    ctxl[...] = jnp.where(row_low, contexts[0], contexts[1]).astype(BF16)

    gather2 = RelayGather(tp, ctxl, ctxf, relay_send.at[1], relay_recv.at[1])
    gather2.start()
    gather2.finish()
    attention = dot_nn(side_by_side(ctxf), outf[...].reshape(nt * width, nt * width))
    residual = side_by_side(visitf).astype(F32) + attention
    scaled2, inverse2, normed2 = norm_rows(residual, gain2[...])
    rgrad[...] = residual
    own = pl.ds(pl.multiple_of(tp.me * width, width), width)
    residual_own[...] = rgrad[:, own]
    upper = dot_nn(normed2, up[...])
    cubic = 0.7978845608028654 * (upper + 0.044715 * upper * upper * upper)
    bend = jnp.tanh(cubic)
    hidden = (0.5 * upper * (1.0 + bend)).astype(BF16)
    slope = 0.5 * (1.0 + bend) + 0.5 * upper * (1.0 - bend * bend) * (
        0.7978845608028654 * (1.0 + 3.0 * 0.044715 * upper * upper)
    )
    upper_grad = (hidden_grad[...] * slope).astype(BF16)
    for t in range(nt):
        part2[t] = dot_nt(upper_grad, up[t * width : (t + 1) * width, :]).astype(BF16)
    reduce2 = Exchange(tp, part2, got2, ex_send.at[0], ex_recv.at[0])
    reduce2.start()
    for t in range(nt):
        partf[t] = dot_nn(hidden, down[:, t * width : (t + 1) * width]).astype(BF16)
    reduce2.finish()
    total = got2[0].astype(F32)
    for t in range(1, nt):
        total = total + got2[t].astype(F32)
    sum2[...] = total.astype(BF16)
    gather3 = RelayGather(tp, sum2, sum2f, relay_send.at[2], relay_recv.at[2])
    gather3.start()
    reducef = Exchange(tp, partf, gotf, ex_send.at[1], ex_recv.at[1])
    gather3.finish()
    reducef.start()

    weighted = side_by_side(sum2f).astype(F32) * gain2[...]
    centred = weighted - jnp.mean(weighted, axis=-1, keepdims=True)
    out_grad = jnp.where(iota((rows, nt * width), 0) < limit, side_by_side(cotf).astype(F32), 0.0)
    residual_grad = out_grad + inverse2 * (
        centred - scaled2 * jnp.mean(weighted * scaled2, axis=-1, keepdims=True)
    )
    rgrad[...] = residual_grad
    context_grad = dot_nt(residual_grad.astype(BF16), outw[...]).astype(BF16)

    q, k, v = (projected[:, j * width : (j + 1) * width] for j in range(3))
    query_grads, key_grads, value_grads = [], [], []
    for h, mask in enumerate((low_b, high_b)):
        prob = vprobs[h]
        weight_grad = dot_nt(context_grad, v * mask)
        value_grads.append(dot_tn(prob.astype(BF16), context_grad))
        score_grad = (
            0.125 * prob * (weight_grad - jnp.sum(weight_grad * prob, axis=-1, keepdims=True))
        ).astype(BF16)
        query_grads.append(dot_nn(score_grad, k))
        key_grads.append(dot_tn(score_grad, q))
    packed = jnp.concatenate(
        [
            jnp.where(row_low, pair[0], pair[1]).astype(BF16)
            for pair in (query_grads, key_grads, value_grads)
        ],
        axis=1,
    )
    first_sum = jnp.zeros((rows, 1), F32)
    second_sum = jnp.zeros((rows, 1), F32)
    for t in range(nt):
        cols = slice(t * width, (t + 1) * width)
        partial = dot_nt(packed, qkv[cols, :])
        part1[t] = partial.astype(BF16)
        weighted = partial * gain1[:, cols]
        first_sum = first_sum + jnp.sum(weighted, axis=-1, keepdims=True)
        second_sum = second_sum + jnp.sum(weighted * scaled1[:, cols], axis=-1, keepdims=True)
    reduce1 = Exchange(tp, part1, got1, ex_send.at[2], ex_recv.at[2])
    reduce1.start()
    lane = iota((rows, width), 1)
    both_sums = jnp.where(lane == 0, first_sum, jnp.where(lane == 1, second_sum, 0.0))
    stat[...] = jnp.transpose(
        jnp.concatenate([both_sums, jnp.zeros((padded - rows, width), F32)], axis=0)
    )[:8]
    gather4 = Exchange(tp, stat, stats, ex_send.at[3], ex_recv.at[3], same=True)
    gather4.start()
    reduce1.finish()
    gather4.finish()
    total = got1[0].astype(F32)
    means = stats[0]
    for t in range(1, nt):
        total = total + got1[t].astype(F32)
        means = means + stats[t]
    means = jnp.transpose(
        jnp.concatenate([means, jnp.zeros((width - 8, padded), F32)], axis=0)
    )[:rows] * (1.0 / (nt * width))
    visit_grad = rgrad[:, own] + inverse1[...] * (
        total * gain1[:, own] - means[:, 0:1] - scaled1[:, own] * means[:, 1:2]
    )
    visit_grad = visit_grad.astype(BF16)
    slots2[...] = dot_nn(place_t[:, :rows], visit_grad).astype(BF16).reshape(nn, lat, width)
    back = AllToAll(nn, slots2, arrived2, a2a_send.at[2], a2a_recv.at[2])
    back.start()

    reducef.finish()
    total = gotf[0].astype(F32)
    for t in range(1, nt):
        total = total + gotf[t].astype(F32)
    visit_out[...] = jnp.where(row_valid, residual_own[...] + total, 0.0).astype(BF16)
    sublane = iota((notes * lat, nn * lat), 0)
    wanted = jnp.zeros((notes * lat, 1), I32)
    column = iota((notes * lat, 1), 0)
    wanted = lax.rem(column, lat)
    for n in range(notes):
        wanted = jnp.where(column // lat == n, wanted + pid[n] * lat, wanted)
    unselect = (iota((notes * lat, nn * lat), 1) == wanted).astype(F32).astype(BF16)
    for gather in (gather1, gather2, gather3):
        gather.drain()
    for exchange in (reduce2, reducef, reduce1, gather4):
        exchange.drain()

    back.finish()
    latent = dot_nn(unselect, arrived2[...].reshape(nn * lat, width)).astype(BF16)
    latent_out[...] = latent
    halves = (latent * low_b, latent * high_b)
    spread = jnp.concatenate(
        [half[n * lat : (n + 1) * lat] for n in range(notes) for half in halves], axis=0
    )
    partial = dot_tn(mixture[...], spread).astype(BF16)
    vpart[...] = partial.reshape(nz, ny, lat, width)
    query_total = jnp.zeros((both, width), F32)
    for n in range(notes):
        here = slice(n * both, (n + 1) * both)
        tokens = slice(n * tok, (n + 1) * tok)
        prob = probs[here, :]
        prob_grad = dot_nt(spread[here], values[tokens, :])
        score_grad = prob * (prob_grad - jnp.sum(prob_grad * prob, axis=-1, keepdims=True))
        query_total = query_total + dot_nn(score_grad.astype(BF16), states[tokens, :])
    qpart[...] = 0.125 * jnp.where(lane_low, query_total[:lat], query_total[lat:])

    y_copies = []
    for s in range(1, ny):
        to = lax.rem(wy + s, ny)
        device = {"notes": wz * ny + to}
        for i, (src, dst) in enumerate(((vpart.at[:, to], vgot.at[wy]), (qpart, qgot.at[wy]))):
            one = remote(src, dst, y_send.at[i, s], y_recv.at[i, wy], device)
            one.start()
            y_copies.append(one)
    total = vpart[:, wy].astype(F32)
    query_sum = qpart[...]
    for s in range(1, ny):
        owner = lax.rem(wy + s, ny)
        device = {"notes": wz * ny + owner}
        for i, (src, dst) in enumerate(((vpart.at[:, owner], vgot.at[owner]), (qpart, qgot.at[owner]))):
            remote(src, dst, y_send.at[i, s], y_recv.at[i, owner], device).wait_recv()
        total = total + vgot[owner].astype(F32)
        query_sum = query_sum + qgot[owner]
    vpart2[...] = total.astype(BF16)
    qpart2[...] = query_sum

    def along_z(k, carry):
        to = lax.rem(wz + k, nz)
        device = {"notes": to * ny + wy}
        remote(vpart2.at[to], vgot2.at[wz], z_send.at[0], z_recv.at[0], device).start()
        remote(qpart2, qgot2.at[wz], z_send.at[1], z_recv.at[1], device).start()
        return carry

    lax.fori_loop(1, nz, along_z, 0)
    vgot2[wz] = vpart2[wz]
    qgot2[wz] = qpart2[...]
    for one in y_copies:
        one.wait_send()
    span = pl.ds(0, nz - 1)
    remote(vpart2.at[span], vgot2.at[span], z_send.at[0], z_recv.at[0], {"notes": who}).wait()
    remote(qgot2.at[span], qgot2.at[span], z_send.at[1], z_recv.at[1], {"notes": who}).wait()
    total = vgot2[0].astype(F32)
    query_sum = qgot2[0]
    for z in range(1, nz):
        total = total + vgot2[z].astype(F32)
        query_sum = query_sum + qgot2[z]
    value_out[...] = total
    query_out[...] = query_sum


def shards(
    mesh_shape,
    states,
    value_weight,
    latent_query,
    patient_ids,
    note_order,
    history_length,
    position_table,
    attention_gain,
    feedforward_gain,
    qkv_weight,
    out_weight,
    up_weight,
    down_weight,
    cotangent,
):
    nn, nt = mesh_shape["notes"], mesh_shape["tensor"]
    ny = 4
    nz = nn // ny
    notes, tok, width = states.shape
    lat, most = latent_query.shape[0], position_table.shape[0]
    rows = most * lat
    dim = nt * width
    inner = up_weight.shape[1]
    padded = -(-rows // 128) * 128
    both = 2 * lat
    dims = (nn, ny, nt, notes, tok, lat, most)
    vmem = pl.BlockSpec(memory_space=pltpu.VMEM)
    smem = pl.BlockSpec(memory_space=pltpu.SMEM)
    hbm = pl.BlockSpec(memory_space=pl.ANY)
    V = pltpu.VMEM
    dma = pltpu.SemaphoreType.DMA
    block = (nt, rows, width)
    scratch = [
        V((dim, width), BF16),
        V((dim, 3 * width), BF16),
        V((dim, inner), BF16),
        V((inner, dim), BF16),
        V((nt, notes * tok, width), BF16),
        V(block, BF16),
        V((nt, width, dim), BF16),
        V((nn, 1, width), I32),
        V((nn, 1, width), I32),
        V((notes * both, tok), F32),
        V((notes * both, tok), BF16),
        V((notes * tok, width), BF16),
        V((notes * both, dim), BF16),
        V((nn, lat, width), BF16),
        V((nn, lat, width), BF16),
        V((nn * lat, padded), BF16),
        V((padded, nn * lat), BF16),
        V((rows, width), BF16),
        V(block, BF16),
        V((rows, dim), F32),
        V((rows, width), F32),
        V((rows, 3 * width), BF16),
        V((2, rows, rows), F32),
        V((rows, width), BF16),
        V(block, BF16),
        V((rows, width), F32),
        V((rows, inner), F32),
        V(block, BF16),
        V(block, BF16),
        V((rows, width), BF16),
        V(block, BF16),
        V(block, BF16),
        V(block, BF16),
        V((rows, dim), F32),
        V(block, BF16),
        V(block, BF16),
        V((8, padded), F32),
        V((nt, 8, padded), F32),
        V((nn, lat, width), BF16),
        V((nn, lat, width), BF16),
        V((nz, ny, lat, width), BF16),
        V((ny, nz, lat, width), BF16),
        V((nz, lat, width), BF16),
        V((nz, lat, width), BF16),
        V((lat, width), F32),
        V((ny, lat, width), F32),
        V((lat, width), F32),
        V((nz, lat, width), F32),
        dma((4,)),
        dma((3, 14)),
        dma((3, nt, 2)),
        dma((3, 7)),
        dma((3, nt)),
        dma((4, nt - 1)),
        dma((4, nt)),
        dma((3,)),
        dma((3,)),
        dma((2, ny)),
        dma((2, ny)),
        dma((2,)),
        dma((2,)),
    ]
    visit_out, latent_grads, value_grad, query_grad = pl.pallas_call(
        functools.partial(body, dims),
        out_shape=(
            jax.ShapeDtypeStruct((rows, width), BF16),
            jax.ShapeDtypeStruct((notes * lat, width), BF16),
            jax.ShapeDtypeStruct((dim // nn, width), F32),
            jax.ShapeDtypeStruct((lat, width), F32),
        ),
        in_specs=[smem] * 3 + [vmem] * 7 + [hbm] * 4,
        out_specs=(vmem,) * 4,
        scratch_shapes=scratch,
        name="note_visit_step",
        compiler_params=pltpu.CompilerParams(
            collective_id=0, has_side_effects=True, vmem_limit_bytes=56 * 2**20
        ),
    )(
        patient_ids,
        note_order,
        history_length,
        states.reshape(notes * tok, width),
        latent_query,
        position_table,
        attention_gain.reshape(1, dim),
        feedforward_gain.reshape(1, dim),
        cotangent.reshape(rows, width),
        out_weight,
        value_weight,
        qkv_weight.reshape(dim, 3 * width),
        up_weight,
        down_weight,
    )
    return (
        visit_out[None],
        latent_grads.reshape(notes, lat, width),
        value_grad,
        query_grad,
    )


def solution(mesh):
    return jax.shard_map(
        functools.partial(shards, dict(mesh.shape)),
        mesh=mesh,
        in_specs=(
            P("notes", None, "tensor"),
            P(None, "tensor"),
            P(None, "tensor"),
            P("notes"),
            P("notes"),
            P("notes"),
            P(None, "tensor"),
            P(),
            P(),
            P(None, None, "tensor"),
            P("tensor", None),
            P(None, "tensor"),
            P("tensor", None),
            P("notes", None, "tensor"),
        ),
        out_specs=(
            P("notes", None, "tensor"),
            P("notes", None, "tensor"),
            P("notes", "tensor"),
            P(None, "tensor"),
        ),
        check_vma=False,
    )
```

time: 1090 us -> 150 us (0.14)
  waiting for transfers between devices: 800 us -> 0 us
  blocking collectives: 176 us -> 0 us
  Pallas kernels: 0 us -> 140 us
  starting transfers between devices: 34.9 us -> 0 us
  matrix products: 23.9 us -> 0 us
  other arithmetic: 16.1 us -> 0 us
  between operations: 15.1 us -> 1.31 us
    unnamed x6 -> x0, waiting for transfers between devices: 559 us -> none
    psum x3 -> x0, waiting for transfers between devices: 203 us -> none  [the longest x1 77.7 us: block_tail(): lax.psum(jnp.dot(hidden, down_weight, preferred_element_type=jnp.float32)...]
    pallas_call x0 -> x1, Pallas kernels: none -> 140 us  [shards(): pl.pallas_call(functools.partial(body, dims), out_shape=(jax.ShapeDtypeSt...]
    psum x1 -> x0, blocking collectives: 115 us -> none  [shards(): lax.psum(query_partial.reshape(latent_count, local_width), 'notes')]
    all_to_all x2 -> x0, starting transfers between devices: 34.6 us -> none  [the longest x1 19.3 us: shards(): lax.all_to_all(order_codes, 'notes', split_axis=0, concat_axis=0, tiled=T...]
    all_to_all x1 -> x0, blocking collectives: 32.4 us -> none  [shards(): lax.all_to_all(owner_send(placement, slot_grads, owners), 'notes', split_...]
    all_gather x2 -> x0, blocking collectives: 28.9 us -> none  [the longest x1 16.1 us: shards(): lax.all_gather(visit_local, 'tensor', axis=1, tiled=True)]
    dot_general x24 -> x0, matrix products: 22.5 us -> none  [the longest x1 3.18 us: block_tail_back(): jnp.einsum('rf,df->rd', upper_grad, up_weight, preferred_element_type=jnp...]
  transfers between devices with their start and end apart: 7 -> 0, of which waited for: 6 -> 0; matrix products, arithmetic and copies ran while one was open for 2% -> 0% of each run, Pallas kernels for 0% -> 0%
where the time goes in v1:
time: 150 us; the launch traced here: 147 us
  Pallas kernels  140 us (93%)
  local copies, waits for them, and re-layouts  6.1 us (4%)
    pallas_call x1, Pallas kernels, shards(): pl.pallas_call(functools.partial(body, dims), out_shape=(jax.ShapeDtypeSt...  140 us
    unnamed x11, local copies, waits for them, and re-layouts  4.94 us

profile of v1, /device:TPU:1, one launch (start us, length us, event | category | flops | bytes accessed | tf_op | source)
XLA Modules:
  0.0 147.2 jit_solution(2896907640615814606)
XLA Ops:
  0.6 1.4 copy.19
  2.0 1.2 copy.20.qkv_hbm
  3.9 139.8 %note_visit_step.1 = (bf16[288,128]{1,0:T(8,128)(2,1)}, bf16[192,128]{1,0:T(8,128)(2,1)}, f32[16,128]{1,0:T(8,128)}, f32[16,128]{1,0:T(8,128)}) custom-call(s32[12]{0:T(128)} %pid.1, s32[12]{0:T(128)} %order.1, s32[1]{0:T(128)S(6)} %copy.25.length, bf16[1536,128]{1,0:T(8,128)(2,1)} %bitcast.8, bf16[16,128]{1,0:T(8,128)(2,1)} %lq.1, bf16[18,128]{1,0:T(8,128)(2,1)} %pos.1, ...), custom_call_target="tpu_custom_call" | custom-call | tf_op jit(solution)/shard_map/note_visit_step/pallas_call | solution.py:742
  143.6 0.0 copy-start
  143.7 1.5 %copy.26 = bf16[1,288,128]{2,1,0:T(8,128)(2,1)} copy(bf16[1,288,128]{2,1,0:T(8,128)(2,1)} %bitcast.9) | data formatting | bytes 147456
  145.2 0.0 copy-done
  145.2 0.0 copy-start.2
  145.2 0.6 copy.27
  145.8 0.1 copy-done.2
  145.9 0.0 copy-start.1
  145.9 0.6 copy.28
  146.5 0.1 copy-done.1
  146.6 0.6 copy.29
Async XLA Ops:
  143.6 1.5 %copy-start = (bf16[192,128]{1,0:T(8,128)(2,1)S(1)}, bf16[192,128]{1,0:T(8,128)(2,1)}, u32[]{:S(2)}) copy-start(bf16[192,128]{1,0:T(8,128)(2,1)} %get-tuple-element.9) | copy-start | bytes 147460
  145.2 0.7 copy-start.2
  145.9 0.7 copy-start.1

commit v2 on v1

--- a/solution.py
+++ b/solution.py
@@ -203,20 +203,87 @@
             one.wait_send()
 
 
+class PairReduce:
+    def __init__(self, place, part, pair, joined, got, send, recv):
+        self.place, self.part, self.pair, self.joined, self.got = place, part, pair, joined, got
+        self.send, self.recv = send, recv
+        self.copies = []
+
+    def start(self, x):
+        p = self.place
+        one = remote(
+            self.part.at[x * 2 + 1 - p.c],
+            self.pair.at[x],
+            self.send.at[x],
+            self.recv.at[x],
+            {"tensor": p.sibling},
+        )
+        one.start()
+        self.copies.append(one)
+
+    def join(self, x):
+        p = self.place
+        remote(
+            self.part.at[x * 2 + p.c],
+            self.pair.at[x],
+            self.send.at[0],
+            self.recv.at[x],
+            {"tensor": p.sibling},
+        ).wait_recv()
+        return self.part[x * 2 + p.c].astype(F32) + self.pair[x].astype(F32)
+
+    def middle(self):
+        p = self.place
+        nx = p.nx
+        for i, step in enumerate((2, 1, 3)):
+            x = lax.rem(p.x + step, nx)
+            self.joined[i] = self.join(x).astype(BF16)
+            one = remote(
+                self.joined.at[i],
+                self.got.at[p.x],
+                self.send.at[nx + i],
+                self.recv.at[nx + p.x],
+                {"tensor": x * 2 + p.c},
+            )
+            one.start()
+            self.copies.append(one)
+
+    def finish(self):
+        p = self.place
+        nx = p.nx
+        total = self.join(p.x)
+        for i, step in enumerate((1, 3, 2)):
+            x = lax.rem(p.x + step, nx)
+            remote(
+                self.joined.at[i],
+                self.got.at[x],
+                self.send.at[nx],
+                self.recv.at[nx + x],
+                {"tensor": x * 2 + p.c},
+            ).wait_recv()
+            total = total + self.got[x].astype(F32)
+        return total
+
+    def drain(self):
+        for one in self.copies:
+            one.wait_send()
+
+
 class AllToAll:
     def __init__(self, count, src, slots, send, recv):
         self.count, self.src, self.slots, self.send, self.recv = count, src, slots, send, recv
         self.me = lax.axis_index("notes")
 
     def start(self):
-        def step(k, carry):
+        def step(j, carry):
+            k = self.count // 2 + (j + 1) // 2 * (1 - 2 * lax.rem(j, 2))
             to = lax.rem(self.me + k, self.count)
             remote(
                 self.src.at[to], self.slots.at[self.me], self.send, self.recv, {"notes": to}
             ).start()
             return carry
 
-        lax.fori_loop(1, self.count, step, 0)
+        lax.fori_loop(0, self.count - 1, step, 0)
         self.slots[self.me] = self.src[self.me]
 
     def finish(self):
@@ -242,13 +309,13 @@
     pid,
     order,
     length,
-    states,
-    lq,
-    pos,
-    gain1,
-    gain2,
-    cot,
-    outw,
+    states_hbm,
+    lq_hbm,
+    pos_hbm,
+    gain1_hbm,
+    gain2_hbm,
+    cot_hbm,
+    outw_hbm,
     wv_hbm,
     qkv_hbm,
     up_hbm,
@@ -257,6 +324,13 @@
     latent_out,
     value_out,
     query_out,
+    states,
+    lq,
+    pos,
+    gain1,
+    gain2,
+    cot,
+    outw,
     wv,
     qkv,
     up,
@@ -283,15 +357,25 @@
     ctxl,
     ctxf,
     residual_own,
+    scaled2,
+    inverse2,
+    hidden,
     hidden_grad,
     part2,
+    pair2,
+    joined2,
     got2,
     sum2,
     sum2f,
+    context_grads,
     partf,
+    pairf,
+    joinedf,
     gotf,
     rgrad,
     part1,
+    pair1,
+    joined1,
     got1,
     stat,
     stats,
@@ -312,6 +396,8 @@
     relay_recv,
     ex_send,
     ex_recv,
+    stat_send,
+    stat_recv,
     a2a_send,
     a2a_recv,
     y_send,
@@ -327,23 +413,40 @@
     who = lax.axis_index("notes")
     wz, wy = who // ny, lax.rem(who, ny)
 
+    loads = [
+        pltpu.make_async_copy(src, dst, load_sem.at[i])
+        for i, (src, dst) in enumerate(
+            (
+                (states_hbm, states),
+                (lq_hbm, lq),
+                (wv_hbm, wv),
+                (pos_hbm, pos),
+                (cot_hbm, cot),
+                (outw_hbm, outw),
+                (qkv_hbm.at[0], qkv.at[:, 0:width]),
+                (qkv_hbm.at[1], qkv.at[:, width : 2 * width]),
+                (qkv_hbm.at[2], qkv.at[:, 2 * width :]),
+                (up_hbm, up),
+                (down_hbm, down),
+                (gain1_hbm, gain1),
+                (gain2_hbm, gain2),
+            )
+        )
+    ]
     barrier = pltpu.get_barrier_semaphore()
 
-    def greet(k, carry):
+    def greet(j, carry):
+        k = nn // 2 + (j + 1) // 2 * (1 - 2 * lax.rem(j, 2))
         pl.semaphore_signal(
             barrier, inc=1, device_id={"notes": lax.rem(who + k, nn)}, device_id_type=MESH
         )
         return carry
 
+    lax.fori_loop(0, nn - 1, greet, 0)
     for k in range(1, nt):
         pl.semaphore_signal(
             barrier, inc=1, device_id={"tensor": lax.rem(tp.me + k, nt)}, device_id_type=MESH
         )
-    lax.fori_loop(1, nn, greet, 0)
-    loads = [
-        pltpu.make_async_copy(src, dst, load_sem.at[i])
-        for i, (src, dst) in enumerate(((wv_hbm, wv), (qkv_hbm, qkv), (up_hbm, up), (down_hbm, down)))
-    ]
     for one in loads:
         one.start()
     pl.semaphore_wait(barrier, nt - 1 + nn - 1)
@@ -351,6 +454,7 @@
     ring_states = RingGather(tp, states, full, ring_send.at[0], ring_recv.at[0])
     ring_cot = RingGather(tp, cot, cotf, ring_send.at[1], ring_recv.at[1])
     ring_out = RingGather(tp, outw, outf, ring_send.at[2], ring_recv.at[2])
+    loads[0].wait()
     ring_states.start()
 
     patient = iota((nn, 1, width), 0)
@@ -359,8 +463,8 @@
         codes = jnp.where(patient == pid[n], order[n] + 1, codes)
     codes_out[...] = codes
     route = AllToAll(nn, codes_out, codes_in, a2a_send.at[0], a2a_recv.at[0])
-    route.start()
-
+
+    loads[1].wait()
     low = (iota((1, width), 1) < HEAD).astype(F32)
     low_b, high_b = low.astype(BF16), (1.0 - low).astype(BF16)
     query = jnp.concatenate([lq[...] * low_b, lq[...] * high_b], axis=0)
@@ -374,12 +478,15 @@
 
     ring_states.pass_on()
     ring_states.relay_near()
+    route.start()
+    ring_states.relay_far()
+    loads[4].wait()
+    loads[5].wait()
     ring_cot.start()
     ring_out.start()
-    ring_states.relay_far()
     ring_states.finish()
 
-    loads[0].wait()
+    loads[2].wait()
     pooled = []
     lane_low = iota((lat, width), 1) < HEAD
     for n in range(notes):
@@ -427,6 +534,7 @@
         mixed = dot_nn(weights[n * both : (n + 1) * both, :], note)
         mixture[n * both : (n + 1) * both, :] = mixed.astype(BF16)
 
+    loads[3].wait()
     limit = length[0] * lat
     row_valid = iota((rows, width), 0) < limit
     positions = pos[...].astype(F32)
@@ -435,9 +543,8 @@
     )
     ring_cot.finish()
     ring_out.finish()
-    loads[1].wait()
-    loads[2].wait()
-    loads[3].wait()
+    for one in loads[6:]:
+        one.wait()
     out_grad = jnp.where(iota((rows, nt * width), 0) < limit, side_by_side(cotf).astype(F32), 0.0)
     hidden_grad[...] = dot_nt(out_grad.astype(BF16), down[...])
 
@@ -445,70 +552,97 @@
     placed = dot_nn(place[...], arrived[...].reshape(nn * lat, width))[:rows]
     vloc[...] = jnp.where(row_valid, placed + positions, 0.0).astype(BF16)
 
-    gather1 = RelayGather(tp, vloc, visitf, relay_send.at[0], relay_recv.at[0])
-    gather1.start()
-    gather1.finish()
-    visit = side_by_side(visitf).astype(F32)
-    scaled, inverse, normed = norm_rows(visit, gain1[...])
-    scaled1[...] = scaled
-    inverse1[...] = jnp.broadcast_to(inverse, (rows, width))
-    projected[...] = dot_nn(normed, qkv[...]).astype(BF16)
+    half = rows // 2
+    spans = [slice(j * half, (j + 1) * half) for j in range(2)]
+
+    def relays(src, whole, k):
+        return [
+            RelayGather(
+                tp,
+                src.at[pl.ds(j * half, half)],
+                whole.at[j],
+                relay_send.at[k, j],
+                relay_recv.at[k, j],
+            )
+            for j in range(2)
+        ]
+
+    gathers1 = relays(vloc, visitf, 0)
+    for gather in gathers1:
+        gather.start()
+    for span, gather, blocks in zip(spans, gathers1, (visitf.at[0], visitf.at[1])):
+        gather.finish()
+        scaled, inverse, normed = norm_rows(side_by_side(blocks).astype(F32), gain1[...])
+        scaled1[span, :] = scaled
+        inverse1[span, :] = jnp.broadcast_to(inverse, (half, width))
+        projected[span, :] = dot_nn(normed, qkv[...]).astype(BF16)
     q, k, v = (projected[:, j * width : (j + 1) * width] for j in range(3))
     key_valid = iota((1, rows), 1) < limit
-    contexts = []
-    for h, mask in enumerate((low_b, high_b)):
-        score = jnp.where(key_valid, 0.125 * dot_nt(q, k * mask), MASKED)
-        score = jnp.exp(score - jnp.max(score, axis=-1, keepdims=True))
-        prob = score / jnp.sum(score, axis=-1, keepdims=True)
-        vprobs[h] = prob
-        contexts.append(dot_nn(prob.astype(BF16), v))
+    gathers2 = relays(ctxl, ctxf, 1)
+    half_low = iota((half, width), 1) < HEAD
+    key_heads = (k * low_b, k * high_b)
+    for span, gather in zip(spans, gathers2):
+        contexts = []
+        for h in range(2):
+            score = jnp.where(key_valid, 0.125 * dot_nt(q[span], key_heads[h]), MASKED)
+            score = jnp.exp(score - jnp.max(score, axis=-1, keepdims=True))
+            prob = score / jnp.sum(score, axis=-1, keepdims=True)
+            vprobs[h, span, :] = prob
+            contexts.append(dot_nn(prob.astype(BF16), v))
+        ctxl[span, :] = jnp.where(half_low, contexts[0], contexts[1]).astype(BF16)
+        gather.start()
+
+    reduces2 = [
+        PairReduce(
+            tp, part2.at[j], pair2.at[j], joined2.at[j], got2.at[j], ex_send.at[j], ex_recv.at[j]
+        )
+        for j in range(2)
+    ]
+    own = pl.ds(pl.multiple_of(tp.me * width, width), width)
+    for j, span in enumerate(spans):
+        gathers2[j].finish()
+        attention = dot_nn(side_by_side(ctxf.at[j]), outf[...].reshape(nt * width, nt * width))
+        residual = side_by_side(visitf.at[j]).astype(F32) + attention
+        scaled, inverse, normed = norm_rows(residual, gain2[...])
+        rgrad[span, :] = residual
+        scaled2[span, :] = scaled
+        inverse2[span, :] = jnp.broadcast_to(inverse, (half, width))
+        upper = dot_nn(normed, up[...])
+        if j:
+            reduces2[0].middle()
+        bend = jnp.tanh(0.7978845608028654 * (upper + 0.044715 * upper * upper * upper))
+        hidden[span, :] = (0.5 * upper * (1.0 + bend)).astype(BF16)
+        slope = 0.5 * (1.0 + bend) + 0.5 * upper * (1.0 - bend * bend) * (
+            0.7978845608028654 * (1.0 + 3.0 * 0.044715 * upper * upper)
+        )
+        upper_grad = (hidden_grad[span, :] * slope).astype(BF16)
+        for x in range(nt // 2):
+            pair = dot_nt(upper_grad, up[2 * x * width : 2 * (x + 1) * width, :]).astype(BF16)
+            part2[j, 2 * x] = pair[:, :width]
+            part2[j, 2 * x + 1] = pair[:, width:]
+            reduces2[j].start(x)
+    reduces2[1].middle()
+    residual_own[...] = rgrad[:, own]
+    gathers3 = relays(sum2, sum2f, 2)
+    for span, reduce, gather in zip(spans, reduces2, gathers3):
+        sum2[span, :] = reduce.finish().astype(BF16)
+        gather.start()
+    for j, span in enumerate(spans):
+        gathers3[j].finish()
+        weighted = side_by_side(sum2f.at[j]).astype(F32) * gain2[...]
+        centred = weighted - jnp.mean(weighted, axis=-1, keepdims=True)
+        given = jnp.concatenate([cotf[t, span, :] for t in range(nt)], axis=1).astype(F32)
+        row = iota((half, nt * width), 0) + j * half
+        scaled = scaled2[span, :]
+        residual_grad = jnp.where(row < limit, given, 0.0) + inverse2[span, 0:1] * (
+            centred - scaled * jnp.mean(weighted * scaled, axis=-1, keepdims=True)
+        )
+        rgrad[span, :] = residual_grad
+        context_grads[span, :] = dot_nt(residual_grad.astype(BF16), outw[...]).astype(BF16)
+
+    q, k, v = (projected[:, j * width : (j + 1) * width] for j in range(3))
+    context_grad = context_grads[...]
     row_low = iota((rows, width), 1) < HEAD
-    ctxl[...] = jnp.where(row_low, contexts[0], contexts[1]).astype(BF16)
-
-    gather2 = RelayGather(tp, ctxl, ctxf, relay_send.at[1], relay_recv.at[1])
-    gather2.start()
-    gather2.finish()
-    attention = dot_nn(side_by_side(ctxf), outf[...].reshape(nt * width, nt * width))
-    residual = side_by_side(visitf).astype(F32) + attention
-    scaled2, inverse2, normed2 = norm_rows(residual, gain2[...])
-    rgrad[...] = residual
-    own = pl.ds(pl.multiple_of(tp.me * width, width), width)
-    residual_own[...] = rgrad[:, own]
-    upper = dot_nn(normed2, up[...])
-    cubic = 0.7978845608028654 * (upper + 0.044715 * upper * upper * upper)
-    bend = jnp.tanh(cubic)
-    hidden = (0.5 * upper * (1.0 + bend)).astype(BF16)
-    slope = 0.5 * (1.0 + bend) + 0.5 * upper * (1.0 - bend * bend) * (
-        0.7978845608028654 * (1.0 + 3.0 * 0.044715 * upper * upper)
-    )
-    upper_grad = (hidden_grad[...] * slope).astype(BF16)
-    for t in range(nt):
-        part2[t] = dot_nt(upper_grad, up[t * width : (t + 1) * width, :]).astype(BF16)
-    reduce2 = Exchange(tp, part2, got2, ex_send.at[0], ex_recv.at[0])
-    reduce2.start()
-    for t in range(nt):
-        partf[t] = dot_nn(hidden, down[:, t * width : (t + 1) * width]).astype(BF16)
-    reduce2.finish()
-    total = got2[0].astype(F32)
-    for t in range(1, nt):
-        total = total + got2[t].astype(F32)
-    sum2[...] = total.astype(BF16)
-    gather3 = RelayGather(tp, sum2, sum2f, relay_send.at[2], relay_recv.at[2])
-    gather3.start()
-    reducef = Exchange(tp, partf, gotf, ex_send.at[1], ex_recv.at[1])
-    gather3.finish()
-    reducef.start()
-
-    weighted = side_by_side(sum2f).astype(F32) * gain2[...]
-    centred = weighted - jnp.mean(weighted, axis=-1, keepdims=True)
-    out_grad = jnp.where(iota((rows, nt * width), 0) < limit, side_by_side(cotf).astype(F32), 0.0)
-    residual_grad = out_grad + inverse2 * (
-        centred - scaled2 * jnp.mean(weighted * scaled2, axis=-1, keepdims=True)
-    )
-    rgrad[...] = residual_grad
-    context_grad = dot_nt(residual_grad.astype(BF16), outw[...]).astype(BF16)
-
-    q, k, v = (projected[:, j * width : (j + 1) * width] for j in range(3))
     query_grads, key_grads, value_grads = [], [], []
     for h, mask in enumerate((low_b, high_b)):
         prob = vprobs[h]
@@ -528,28 +662,28 @@
     )
     first_sum = jnp.zeros((rows, 1), F32)
     second_sum = jnp.zeros((rows, 1), F32)
-    for t in range(nt):
-        cols = slice(t * width, (t + 1) * width)
+    reduce1 = PairReduce(tp, part1, pair1, joined1, got1, ex_send.at[2], ex_recv.at[2])
+    for x in range(nt // 2):
+        cols = slice(2 * x * width, 2 * (x + 1) * width)
         partial = dot_nt(packed, qkv[cols, :])
-        part1[t] = partial.astype(BF16)
+        part1[2 * x] = partial[:, :width].astype(BF16)
+        part1[2 * x + 1] = partial[:, width:].astype(BF16)
+        reduce1.start(x)
         weighted = partial * gain1[:, cols]
         first_sum = first_sum + jnp.sum(weighted, axis=-1, keepdims=True)
         second_sum = second_sum + jnp.sum(weighted * scaled1[:, cols], axis=-1, keepdims=True)
-    reduce1 = Exchange(tp, part1, got1, ex_send.at[2], ex_recv.at[2])
-    reduce1.start()
+    reduce1.middle()
     lane = iota((rows, width), 1)
     both_sums = jnp.where(lane == 0, first_sum, jnp.where(lane == 1, second_sum, 0.0))
     stat[...] = jnp.transpose(
         jnp.concatenate([both_sums, jnp.zeros((padded - rows, width), F32)], axis=0)
     )[:8]
-    gather4 = Exchange(tp, stat, stats, ex_send.at[3], ex_recv.at[3], same=True)
+    gather4 = Exchange(tp, stat, stats, stat_send, stat_recv, same=True)
     gather4.start()
-    reduce1.finish()
+    total = reduce1.finish()
     gather4.finish()
-    total = got1[0].astype(F32)
     means = stats[0]
     for t in range(1, nt):
-        total = total + got1[t].astype(F32)
         means = means + stats[t]
     means = jnp.transpose(
         jnp.concatenate([means, jnp.zeros((width - 8, padded), F32)], axis=0)
@@ -562,22 +696,22 @@
     back = AllToAll(nn, slots2, arrived2, a2a_send.at[2], a2a_recv.at[2])
     back.start()
 
-    reducef.finish()
-    total = gotf[0].astype(F32)
-    for t in range(1, nt):
-        total = total + gotf[t].astype(F32)
-    visit_out[...] = jnp.where(row_valid, residual_own[...] + total, 0.0).astype(BF16)
-    sublane = iota((notes * lat, nn * lat), 0)
-    wanted = jnp.zeros((notes * lat, 1), I32)
+    reducef = PairReduce(tp, partf, pairf, joinedf, gotf, ex_send.at[3], ex_recv.at[3])
+    for x in range(nt // 2):
+        pair = dot_nn(hidden[...], down[:, 2 * x * width : 2 * (x + 1) * width]).astype(BF16)
+        partf[2 * x] = pair[:, :width]
+        partf[2 * x + 1] = pair[:, width:]
+        reducef.start(x)
+    reducef.middle()
     column = iota((notes * lat, 1), 0)
     wanted = lax.rem(column, lat)
     for n in range(notes):
         wanted = jnp.where(column // lat == n, wanted + pid[n] * lat, wanted)
     unselect = (iota((notes * lat, nn * lat), 1) == wanted).astype(F32).astype(BF16)
-    for gather in (gather1, gather2, gather3):
-        gather.drain()
-    for exchange in (reduce2, reducef, reduce1, gather4):
-        exchange.drain()
+    total = reducef.finish()
+    visit_out[...] = jnp.where(row_valid, residual_own[...] + total, 0.0).astype(BF16)
+    for one in gathers1 + gathers2 + gathers3 + reduces2 + [reduce1, reducef, gather4]:
+        one.drain()
 
     back.finish()
     latent = dot_nn(unselect, arrived2[...].reshape(nn * lat, width)).astype(BF16)
@@ -616,16 +750,16 @@
         total = total + vgot[owner].astype(F32)
         query_sum = query_sum + qgot[owner]
     vpart2[...] = total.astype(BF16)
-    qpart2[...] = query_sum
-
-    def along_z(k, carry):
-        to = lax.rem(wz + k, nz)
+    qpart2[...] = query_sum.astype(BF16)
+
+    def along_z(j, carry):
+        to = lax.rem(wz + nz // 2 + (j + 1) // 2 * (1 - 2 * lax.rem(j, 2)), nz)
         device = {"notes": to * ny + wy}
         remote(vpart2.at[to], vgot2.at[wz], z_send.at[0], z_recv.at[0], device).start()
         remote(qpart2, qgot2.at[wz], z_send.at[1], z_recv.at[1], device).start()
         return carry
 
-    lax.fori_loop(1, nz, along_z, 0)
+    lax.fori_loop(0, nz - 1, along_z, 0)
     vgot2[wz] = vpart2[wz]
     qgot2[wz] = qpart2[...]
     for one in y_copies:
@@ -634,12 +768,17 @@
     remote(vpart2.at[span], vgot2.at[span], z_send.at[0], z_recv.at[0], {"notes": who}).wait()
     remote(qgot2.at[span], qgot2.at[span], z_send.at[1], z_recv.at[1], {"notes": who}).wait()
     total = vgot2[0].astype(F32)
-    query_sum = qgot2[0]
+    query_sum = qgot2[0].astype(F32)
     for z in range(1, nz):
         total = total + vgot2[z].astype(F32)
-        query_sum = query_sum + qgot2[z]
+        query_sum = query_sum + qgot2[z].astype(F32)
     value_out[...] = total
     query_out[...] = query_sum
+
+
+def hand_over(a, b, c, d, a_out, b_out, c_out, d_out):
+    for src, dst in ((a, a_out), (b, b_out), (c, c_out), (d, d_out)):
+        dst[...] = src[...]
 
 
 def shards(
@@ -676,7 +815,16 @@
     V = pltpu.VMEM
     dma = pltpu.SemaphoreType.DMA
     block = (nt, rows, width)
+    halves = (2, nt, rows // 2, width)
+    nx = nt // 2
     scratch = [
+        V((notes * tok, width), BF16),
+        V((lat, width), BF16),
+        V((most, width), BF16),
+        V((1, dim), F32),
+        V((1, dim), F32),
+        V((rows, width), BF16),
+        V((width, dim), BF16),
         V((dim, width), BF16),
         V((dim, 3 * width), BF16),
         V((dim, inner), BF16),
@@ -695,24 +843,34 @@
         V((nn * lat, padded), BF16),
         V((padded, nn * lat), BF16),
         V((rows, width), BF16),
-        V(block, BF16),
+        V(halves, BF16),
         V((rows, dim), F32),
         V((rows, width), F32),
         V((rows, 3 * width), BF16),
         V((2, rows, rows), F32),
         V((rows, width), BF16),
-        V(block, BF16),
+        V(halves, BF16),
         V((rows, width), F32),
+        V((rows, dim), F32),
+        V((rows, width), F32),
+        V((rows, inner), BF16),
         V((rows, inner), F32),
-        V(block, BF16),
-        V(block, BF16),
+        V(halves, BF16),
+        V((2, nx, rows // 2, width), BF16),
+        V((2, nx - 1, rows // 2, width), BF16),
+        V((2, nx, rows // 2, width), BF16),
+        V((rows, width), BF16),
+        V(halves, BF16),
         V((rows, width), BF16),
         V(block, BF16),
-        V(block, BF16),
-        V(block, BF16),
+        V((nx, rows, width), BF16),
+        V((nx - 1, rows, width), BF16),
+        V((nx, rows, width), BF16),
         V((rows, dim), F32),
         V(block, BF16),
-        V(block, BF16),
+        V((nx, rows, width), BF16),
+        V((nx - 1, rows, width), BF16),
+        V((nx, rows, width), BF16),
         V((8, padded), F32),
         V((nt, 8, padded), F32),
         V((nn, lat, width), BF16),
@@ -723,15 +881,17 @@
         V((nz, lat, width), BF16),
         V((lat, width), F32),
         V((ny, lat, width), F32),
-        V((lat, width), F32),
-        V((nz, lat, width), F32),
-        dma((4,)),
+        V((lat, width), BF16),
+        V((nz, lat, width), BF16),
+        dma((13,)),
         dma((3, 14)),
         dma((3, nt, 2)),
-        dma((3, 7)),
-        dma((3, nt)),
+        dma((3, 2, 7)),
+        dma((3, 2, nt)),
         dma((4, nt - 1)),
         dma((4, nt)),
+        dma((nt - 1,)),
+        dma((nt,)),
         dma((3,)),
         dma((3,)),
         dma((2, ny)),
@@ -747,7 +907,7 @@
             jax.ShapeDtypeStruct((dim // nn, width), F32),
             jax.ShapeDtypeStruct((lat, width), F32),
         ),
-        in_specs=[smem] * 3 + [vmem] * 7 + [hbm] * 4,
+        in_specs=[smem] * 3 + [hbm] * 11,
         out_specs=(vmem,) * 4,
         scratch_shapes=scratch,
         name="note_visit_step",
@@ -766,10 +926,18 @@
         cotangent.reshape(rows, width),
         out_weight,
         value_weight,
-        qkv_weight.reshape(dim, 3 * width),
+        jnp.transpose(qkv_weight, (1, 0, 2)),
         up_weight,
         down_weight,
     )
+    results = (visit_out, latent_grads, value_grad, query_grad)
+    visit_out, latent_grads, value_grad, query_grad = pl.pallas_call(
+        hand_over,
+        out_shape=tuple(jax.ShapeDtypeStruct(r.shape, r.dtype) for r in results),
+        in_specs=[vmem] * 4,
+        out_specs=(vmem,) * 4,
+        name="hand_over",
+    )(*results)
     return (
         visit_out[None],
         latent_grads.reshape(notes, lat, width),

time: 150 us -> 128 us (0.85); the launches traced: 147 us -> 128 us
  Pallas kernels: 140 us -> 126 us
  local copies, waits for them, and re-layouts: 6.1 us -> 0 us
    pallas_call x1, Pallas kernels: 140 us -> 125 us  [shards(): pl.pallas_call(functools.partial(body, dims), out_shape=(jax.ShapeDtypeSt...]
    unnamed x11 -> x0, local copies, waits for them, and re-layouts: 4.94 us -> none
    pallas_call x0 -> x1, Pallas kernels: none -> 1.58 us  [shards(): pl.pallas_call(hand_over, out_shape=tuple((jax.ShapeDtypeStruct(r.shape,...]
where the time goes in v2:
time: 128 us
  Pallas kernels  126 us (98%)
  between operations  1.29 us (1%)
    pallas_call x1, Pallas kernels, shards(): pl.pallas_call(functools.partial(body, dims), out_shape=(jax.ShapeDtypeSt...  125 us

profile of v2, /device:TPU:1, one launch (start us, length us, event | category | flops | bytes accessed | tf_op | source)
XLA Modules:
  0.0 127.8 jit_solution(12529243055659718537)
XLA Ops:
  1.3 124.9 %note_visit_step.1 = (bf16[288,128]{1,0:T(8,128)(2,1)}, bf16[192,128]{1,0:T(8,128)(2,1)}, f32[16,128]{1,0:T(8,128)}, f32[16,128]{1,0:T(8,128)}) custom-call(s32[12]{0:T(128)} %pid.1, s32[12]{0:T(128)} %order.1, s32[1]{0:T(128)S(6)} %copy.18.length, bf16[1536,128]{1,0:T(8,128)(2,1)} %bitcast.8, bf16[16,128]{1,0:T(8,128)(2,1)} %lq_hbm.1, ...), custom_call_target="tpu_custom_call" | custom-call | tf_op jit(solution)/shard_map/note_visit_step/pallas_call | solution.py:902
  126.2 1.6 %hand_over.1 = (bf16[288,128]{1,0:T(8,128)(2,1)}, bf16[192,128]{1,0:T(8,128)(2,1)}, f32[16,128]{1,0:T(8,128)}, f32[16,128]{1,0:T(8,128)}) custom-call(bf16[288,128]{1,0:T(8,128)(2,1)} %get-tuple-element.12.a, bf16[192,128]{1,0:T(8,128)(2,1)} %get-tuple-element.13.b, f32[16,128]{1,0:T(8,128)} %get-tuple-element.14.c, f32[16,128]{1,0:T(8,128)} %get-tuple-element.15.d), custom_call_target="tpu_custom_call" | custom-call | tf_op jit(solution)/shard_map/hand_over/pallas_call | solution.py:934

commit v3 on v2

--- a/solution.py
+++ b/solution.py
@@ -89,9 +89,16 @@
     def start(self):
         p = self.place
         right, left = p.at(1, 0), p.at(3, 0)
-        for j, to in ((0, right), (1, left), (1, right), (0, left), (0, p.sibling), (1, p.sibling)):
+        for j, to in ((0, right), (1, left), (0, p.sibling), (1, p.sibling)):
             self.copy(self.part(self.src, j), p.me, j, to)
         self.full[p.me] = self.src[...]
+
+    def second(self):
+        p = self.place
+        for one in self.copies[:2]:
+            one.wait_send()
+        for j, to in ((1, p.at(1, 0)), (0, p.at(3, 0))):
+            self.copy(self.part(self.src, j), p.me, j, to)
 
     def pass_on(self):
         p = self.place
@@ -117,7 +124,7 @@
         for step in (0, 1, 3, 2):
             for j in range(2):
                 self.arrive(self.place.at(step, 1), j)
-        for one in self.copies:
+        for one in self.copies[2:]:
             one.wait_send()
 
 
@@ -447,7 +454,7 @@
         pl.semaphore_signal(
             barrier, inc=1, device_id={"tensor": lax.rem(tp.me + k, nt)}, device_id_type=MESH
         )
-    for one in loads:
+    for one in loads[:2]:
         one.start()
     pl.semaphore_wait(barrier, nt - 1 + nn - 1)
 
@@ -456,6 +463,8 @@
     ring_out = RingGather(tp, outw, outf, ring_send.at[2], ring_recv.at[2])
     loads[0].wait()
     ring_states.start()
+    for one in loads[2:]:
+        one.start()
 
     patient = iota((nn, 1, width), 0)
     codes = jnp.zeros((nn, 1, width), I32)
@@ -476,6 +485,7 @@
         probs[n * both : (n + 1) * both, :] = prob
         weights[n * both : (n + 1) * both, :] = prob.astype(BF16)
 
+    ring_states.second()
     ring_states.pass_on()
     ring_states.relay_near()
     route.start()
@@ -484,6 +494,8 @@
     loads[5].wait()
     ring_cot.start()
     ring_out.start()
+    ring_cot.second()
+    ring_out.second()
     ring_states.finish()
 
     loads[2].wait()
@@ -528,11 +540,12 @@
     place_t[...] = placing.astype(BF16)
     place[...] = jnp.transpose(placing).astype(BF16)
 
+    mixed = []
     for n in range(notes):
         here = pl.ds(n * tok, tok)
         note = jnp.concatenate([full[t, here, :] for t in range(nt)], axis=1)
-        mixed = dot_nn(weights[n * both : (n + 1) * both, :], note)
-        mixture[n * both : (n + 1) * both, :] = mixed.astype(BF16)
+        mixed.append(dot_nn(weights[n * both : (n + 1) * both, :], note))
+    mixture[...] = jnp.transpose(jnp.concatenate(mixed, axis=0)).astype(BF16)
 
     loads[3].wait()
     limit = length[0] * lat
@@ -669,10 +682,12 @@
         part1[2 * x] = partial[:, :width].astype(BF16)
         part1[2 * x + 1] = partial[:, width:].astype(BF16)
         reduce1.start(x)
-        weighted = partial * gain1[:, cols]
+    reduce1.middle()
+    for t in range(nt):
+        cols = slice(t * width, (t + 1) * width)
+        weighted = part1[t].astype(F32) * gain1[:, cols]
         first_sum = first_sum + jnp.sum(weighted, axis=-1, keepdims=True)
         second_sum = second_sum + jnp.sum(weighted * scaled1[:, cols], axis=-1, keepdims=True)
-    reduce1.middle()
     lane = iota((rows, width), 1)
     both_sums = jnp.where(lane == 0, first_sum, jnp.where(lane == 1, second_sum, 0.0))
     stat[...] = jnp.transpose(
@@ -720,8 +735,50 @@
     spread = jnp.concatenate(
         [half[n * lat : (n + 1) * lat] for n in range(notes) for half in halves], axis=0
     )
-    partial = dot_tn(mixture[...], spread).astype(BF16)
+    partial = dot_nn(mixture[...], spread).astype(BF16)
     vpart[...] = partial.reshape(nz, ny, lat, width)
+    y_copies = []
+
+    def along_y(i, block, slots_y):
+        for s in range(1, ny):
+            to = lax.rem(wy + s, ny)
+            one = remote(
+                block(to),
+                slots_y.at[wy],
+                y_send.at[i, s],
+                y_recv.at[i, wy],
+                {"notes": wz * ny + to},
+            )
+            one.start()
+            y_copies.append(one)
+
+    def from_y(i, s, block, slots_y):
+        owner = lax.rem(wy + s, ny)
+        remote(
+            block(owner),
+            slots_y.at[owner],
+            y_send.at[i, s],
+            y_recv.at[i, owner],
+            {"notes": wz * ny + owner},
+        ).wait_recv()
+        return slots_y[owner].astype(F32)
+
+    def along_z(i, block, slots_z):
+        def step(j, carry):
+            to = lax.rem(wz + nz // 2 + (j + 1) // 2 * (1 - 2 * lax.rem(j, 2)), nz)
+            device = {"notes": to * ny + wy}
+            remote(block(to), slots_z.at[wz], z_send.at[i], z_recv.at[i], device).start()
+            return carry
+
+        lax.fori_loop(0, nz - 1, step, 0)
+
+    def value_block(to):
+        return vpart.at[:, to]
+
+    def query_block(to):
+        return qpart
+
+    along_y(0, value_block, vgot)
     query_total = jnp.zeros((both, width), F32)
     for n in range(notes):
         here = slice(n * both, (n + 1) * both)
@@ -732,34 +789,17 @@
         query_total = query_total + dot_nn(score_grad.astype(BF16), states[tokens, :])
     qpart[...] = 0.125 * jnp.where(lane_low, query_total[:lat], query_total[lat:])
 
-    y_copies = []
+    along_y(1, query_block, qgot)
+    total = vpart[:, wy].astype(F32)
     for s in range(1, ny):
-        to = lax.rem(wy + s, ny)
-        device = {"notes": wz * ny + to}
-        for i, (src, dst) in enumerate(((vpart.at[:, to], vgot.at[wy]), (qpart, qgot.at[wy]))):
-            one = remote(src, dst, y_send.at[i, s], y_recv.at[i, wy], device)
-            one.start()
-            y_copies.append(one)
-    total = vpart[:, wy].astype(F32)
+        total = total + from_y(0, s, value_block, vgot)
+    vpart2[...] = total.astype(BF16)
+    along_z(0, lambda to: vpart2.at[to], vgot2)
     query_sum = qpart[...]
     for s in range(1, ny):
-        owner = lax.rem(wy + s, ny)
-        device = {"notes": wz * ny + owner}
-        for i, (src, dst) in enumerate(((vpart.at[:, owner], vgot.at[owner]), (qpart, qgot.at[owner]))):
-            remote(src, dst, y_send.at[i, s], y_recv.at[i, owner], device).wait_recv()
-        total = total + vgot[owner].astype(F32)
-        query_sum = query_sum + qgot[owner]
-    vpart2[...] = total.astype(BF16)
+        query_sum = query_sum + from_y(1, s, query_block, qgot)
     qpart2[...] = query_sum.astype(BF16)
-
-    def along_z(j, carry):
-        to = lax.rem(wz + nz // 2 + (j + 1) // 2 * (1 - 2 * lax.rem(j, 2)), nz)
-        device = {"notes": to * ny + wy}
-        remote(vpart2.at[to], vgot2.at[wz], z_send.at[0], z_recv.at[0], device).start()
-        remote(qpart2, qgot2.at[wz], z_send.at[1], z_recv.at[1], device).start()
-        return carry
-
-    lax.fori_loop(0, nz - 1, along_z, 0)
+    along_z(1, lambda to: qpart2, qgot2)
     vgot2[wz] = vpart2[wz]
     qgot2[wz] = qpart2[...]
     for one in y_copies:
@@ -837,7 +877,7 @@
         V((notes * both, tok), F32),
         V((notes * both, tok), BF16),
         V((notes * tok, width), BF16),
-        V((notes * both, dim), BF16),
+        V((dim, notes * both), BF16),
         V((nn, lat, width), BF16),
         V((nn, lat, width), BF16),
         V((nn * lat, padded), BF16),

time: 128 us -> 128 us (level); the launches traced: 128 us -> 125 us
  Pallas kernels: 126 us -> 124 us
    pallas_call x1, Pallas kernels: 125 us -> 122 us  [shards(): pl.pallas_call(functools.partial(body, dims), out_shape=(jax.ShapeDtypeSt...]
where the time goes in v3:
time: 128 us; the launch traced here: 125 us
  Pallas kernels  124 us (97%)
  between operations  1.29 us (1%)
    pallas_call x1, Pallas kernels, shards(): pl.pallas_call(functools.partial(body, dims), out_shape=(jax.ShapeDtypeSt...  122 us

profile of v3, /device:TPU:1, one launch (start us, length us, event | category | flops | bytes accessed | tf_op | source)
XLA Modules:
  0.0 125.1 jit_solution(12266050484570875395)
XLA Ops:
  1.3 122.2 %note_visit_step.1 = (bf16[288,128]{1,0:T(8,128)(2,1)}, bf16[192,128]{1,0:T(8,128)(2,1)}, f32[16,128]{1,0:T(8,128)}, f32[16,128]{1,0:T(8,128)}) custom-call(s32[12]{0:T(128)} %pid.1, s32[12]{0:T(128)} %order.1, s32[1]{0:T(128)S(6)} %copy.18.length, bf16[1536,128]{1,0:T(8,128)(2,1)} %bitcast.8, bf16[16,128]{1,0:T(8,128)(2,1)} %lq_hbm.1, ...), custom_call_target="tpu_custom_call" | custom-call | tf_op jit(solution)/shard_map/note_visit_step/pallas_call | solution.py:942
  123.5 1.6 %hand_over.1 = (bf16[288,128]{1,0:T(8,128)(2,1)}, bf16[192,128]{1,0:T(8,128)(2,1)}, f32[16,128]{1,0:T(8,128)}, f32[16,128]{1,0:T(8,128)}) custom-call(bf16[288,128]{1,0:T(8,128)(2,1)} %get-tuple-element.12.a, bf16[192,128]{1,0:T(8,128)(2,1)} %get-tuple-element.13.b, f32[16,128]{1,0:T(8,128)} %get-tuple-element.14.c, f32[16,128]{1,0:T(8,128)} %get-tuple-element.15.d), custom_call_target="tpu_custom_call" | custom-call | tf_op jit(solution)/shard_map/hand_over/pallas_call | solution.py:974
